TPU v7x, 32 devices: a whole 2x2x4 slice. The times are simulated.
32 devices in a mesh: grp: 4 (over y, x), seq: 8 (over z, core).
Axes of the slice: x: 2, y: 2, z: 4, core: 2. Of those that a mesh axis runs over, the one named last changes fastest.
Arguments:
- fake_tokens: bfloat16 [4, 1536, 1536], P('grp', 'seq'), may hold values from -16 to 16
- real_tokens: bfloat16 [4, 1536, 1536], P('grp', 'seq'), may hold values from -6 to 6
- proj_weight: bfloat16 [1536, 2048], P('seq'), may hold values from -0.15625 to 0.15625
- score_vector: float32 [2048], replicated, may hold values from -0.25 to 0.25
Outputs:
- grad_weight: float32 [1536, 2048], P('seq')
All inputs are finite; a program needn't handle non-finite values.
Results may differ from a plain program's by a relative error of at most 0.0003.
Values may be sent and summed in bfloat16 or wider, within the bound.
A program may use at most 64 MiB of HBM per device.

v0:
```python
import math

import jax
import jax.numpy as jnp
from jax import lax
from jax.sharding import PartitionSpec as P

R1_WEIGHT = 40.0


def per_device(fake_tokens, real_tokens, proj_weight, score_vector):
    fake_rows = fake_tokens[0]
    real_rows = real_tokens[0]
    tok_count = fake_rows.shape[0]
    hid_width = proj_weight.shape[1]
    loss_scale = math.sqrt(hid_width / (lax.axis_size("grp") * lax.axis_size("seq") * tok_count))
    joined = jnp.concatenate([fake_rows, real_rows], 0)
    shard_rows = lax.all_gather(proj_weight, "seq", axis=0, tiled=True)
    partial_pre = jnp.dot(joined, shard_rows, preferred_element_type=jnp.float32)
    full_weight = shard_rows
    preact, full_weight = (partial_pre, full_weight)
    squash = jax.nn.sigmoid(preact)
    slopes = squash * (1.0 + preact * (1.0 - squash))
    curves = squash * (1.0 - squash) * (2.0 + preact * (1.0 - 2.0 * squash))
    logits = jnp.dot(preact * squash, score_vector, precision=lax.Precision.HIGHEST)
    slopes_real = slopes[tok_count:]
    lifted = (slopes_real * score_vector).astype(jnp.bfloat16)
    input_grad = lax.dot_general(
        lifted, full_weight, (((1,), (1,)), ((), ())), preferred_element_type=jnp.float32
    )
    r1_cot = (loss_scale * R1_WEIGHT * input_grad).astype(jnp.bfloat16)
    back_grad = jnp.dot(r1_cot, full_weight, preferred_element_type=jnp.float32)
    fake_cot = (
        loss_scale * jax.nn.sigmoid(logits[:tok_count])[:, None] * slopes[:tok_count] * score_vector
    ).astype(jnp.bfloat16)
    real_cot = (
        -loss_scale * jax.nn.sigmoid(-logits[tok_count:])[:, None] * slopes_real * score_vector
        + back_grad * score_vector * curves[tok_count:]
    ).astype(jnp.bfloat16)
    left_rows = jnp.concatenate([fake_rows, real_rows, r1_cot], 0)
    right_rows = jnp.concatenate([fake_cot, real_cot, lifted], 0)
    grad_term = lax.dot_general(
        left_rows, right_rows, (((0,), (0,)), ((), ())), preferred_element_type=jnp.float32
    )
    grad_shard = lax.psum_scatter(grad_term, "seq", scatter_dimension=0, tiled=True)
    return lax.psum(grad_shard, "grp")


def solution(mesh):
    in_specs = (P("grp", "seq", None), P("grp", "seq", None), P("seq", None), P())
    out_specs = P("seq", None)
    return jax.shard_map(
        per_device, mesh=mesh, in_specs=in_specs, out_specs=out_specs, check_vma=False
    )
```

profile of v0, /device:TPU:0, one launch (start us, length us, event | category | flops | bytes accessed | tf_op | source)
XLA Modules:
  0.0 297.6 jit_solution(3272261090798178490)
XLA Ops:
  6.5 0.0 all-gather.2.cloned.1.call-start
  6.5 0.7 all-gather.2.cloned.1.call-update
  7.3 0.0 reduce-scatter.2.cloned.1.call-start
  7.3 69.2 %all-gather.2.cloned.1.call-done = bf16[1536,2048]{1,0:T(8,128)(2,1)} async-done(((bf16[192,2048]{1,0:T(8,128)(2,1)}), bf16[1536,2048]{1,0:T(8,128)(2,1)}) %all-gather.2.cloned.1.call-update) | async-done | bytes 6291472 | tf_op jit(solution)/shard_map/all_gather | solution.py:18
  76.5 0.0 copy-start
  76.5 5.6 %add_divide_fusion = (f32[384,2048]{1,0:T(8,128)S(1)}, f32[384,2048]{1,0:T(8,128)S(1)}, f32[384,2048]{1,0:T(8,128)S(1)}, f32[384,2048]{1,0:T(8,128)S(1)}) fusion(bf16[1536,2048]{1,0:T(8,128)(2,1)} %all-gather.2.cloned.1.call-done, bf16[192,1536]{1,0:T(8,128)(2,1)} %bitcast.12, bf16[192,1536]{1,0:T(8,128)(2,1)} %bitcast.14), kind=kOutput, calls=%fused_computation.3 | convolution fusion | flops 2423783424 | bytes 20054016 | tf_op jit(solution)/shard_map/dot_general | solution.py:19
  82.1 0.0 slice-start
  82.1 0.0 copy-done
  82.1 0.0 slice-start.1
  82.1 3.3 %fusion.25 = f32[384]{0:T(512)S(1)} fusion(f32[2048,1]{0,1:T(1,128)S(1)} %bitcast.9, f32[384,2048]{1,0:T(8,128)S(1)} %get-tuple-element.12), kind=kOutput, calls=%fused_computation.34 | convolution fusion | flops 12582912 | bytes 3155456 | tf_op jit(solution)/shard_map/dot_general | solution.py:25
  85.4 0.1 divide_multiply_fusion.1
  85.5 0.3 fusion.20
  85.8 0.0 slice-done
  85.9 0.0 slice-done.1
  85.9 2.2 fusion.5
  88.1 0.0 copy-start.1
  88.1 0.0 copy-start.2
  88.1 1.8 fusion.4
  89.9 0.0 copy-done.1
  90.0 0.0 copy-done.2
  90.0 8.0 %fusion.6 = f32[1536,2048]{1,0:T(8,128)} fusion(bf16[192,2048]{1,0:T(8,128)(2,1)S(1)} %get-tuple-element.6, bf16[192,2048]{1,0:T(8,128)(2,1)S(1)} %fusion.4, bf16[192,2048]{1,0:T(8,128)(2,1)S(1)} %get-tuple-element.5, bf16[192,1536]{1,0:T(8,128)(2,1)S(1)} %fusion.5, bf16[192,1536]{1,0:T(8,128)(2,1)S(1)} %bitcast.13, bf16[192,1536]{1,0:T(8,128)(2,1)S(1)} %bitcast.15), kind=kOutput, calls=%fused_computation.10 | convolution fusion | flops 3636264960 | bytes 16711680 | tf_op jit(solution)/shard_map/dot_general | solution.py:42
  98.0 0.0 reduce-scatter.2.cloned.1.call-update
  98.0 0.0 all-reduce.2.cloned.1.call-start
  98.0 128.0 %reduce-scatter.2.cloned.1.call-done = f32[192,2048]{1,0:T(8,128)} async-done(((f32[1536,2048]{1,0:T(8,128)}), f32[192,2048]{1,0:T(8,128)}) %reduce-scatter.2.cloned.1.call-update) | async-done | bytes 1572880 | tf_op jit(solution)/shard_map/reduce_scatter | solution.py:45
  226.0 0.0 all-reduce.2.cloned.1.call-update
  226.0 62.4 %all-reduce.2.cloned.1.call-done = f32[192,2048]{1,0:T(8,128)} async-done(((f32[192,2048]{1,0:T(8,128)}), f32[192,2048]{1,0:T(8,128)}) %all-reduce.2.cloned.1.call-update) | async-done | bytes 1572880 | tf_op jit(solution)/shard_map/psum | solution.py:46
  288.4 2.7 copy.6
  (1 shorter events, 0.0 us)
Async XLA Ops:
  6.5 70.0 %all-gather.2.cloned.1.call-start = ((), (), s32[]{:S(2)}) async-start(), calls=%async_computation.1 | async-start | bytes 7077888 | tf_op jit(solution)/shard_map/all_gather | solution.py:18
  7.3 218.8 %reduce-scatter.2.cloned.1.call-start = ((), (), s32[]{:S(2)}) async-start(), calls=%async_computation.2 | async-start | bytes 14155776 | tf_op jit(solution)/shard_map/reduce_scatter | solution.py:45
  76.5 5.6 %copy-start = (f32[2048]{0:T(1024)S(1)}, f32[2048]{0:T(1024)}, u32[]{:S(2)}) copy-start(f32[2048]{0:T(1024)} %param.7) | copy-start | bytes 24580
  82.1 3.7 %slice-start = ((s8[6291456]{0:T(1024)(128)(4,1)}), s8[4194304]{0:T(1024)(128)(4,1)S(1)}, s32[]{:S(2)}) async-start(s8[6291456]{0:T(1024)(128)(4,1)} %bitcast.10), calls=%async_computation.4 | async-start | bytes 8388608
  82.1 3.7 %slice-start.1 = ((s8[6291456]{0:T(1024)(128)(4,1)}), s8[2097152]{0:T(1024)(128)(4,1)S(1)}, s32[]{:S(2)}) async-start(s8[6291456]{0:T(1024)(128)(4,1)} %bitcast.10), calls=%async_computation.5 | async-start | bytes 4194304
  88.1 1.9 copy-start.1
  88.1 1.9 copy-start.2
  98.0 190.4 %all-reduce.2.cloned.1.call-start = ((), (), s32[]{:S(2)}) async-start(), calls=%async_computation.3 | async-start | bytes 3145728 | tf_op jit(solution)/shard_map/psum | solution.py:46
Sparse Core Ops, SparseCore 0:
  9.0 67.4 all-gather.1
  98.1 127.8 reduce-scatter.1
  229.1 59.2 all-reduce.1
where the time goes:
time: 298 us
  waiting for transfers between devices  260 us (87%)
  matrix products  20.9 us (7%)
  between operations  13.2 us (4%)
    reduce_scatter x1, waiting for transfers between devices, per_device(): lax.psum_scatter(grad_term, 'seq', scatter_dimension=0, tiled=True)  128 us
    all_gather x1, waiting for transfers between devices, per_device(): shard_rows = lax.all_gather(proj_weight, 'seq', axis=0, tiled=True)  69.2 us
    psum x1, waiting for transfers between devices, per_device(): return lax.psum(grad_shard, 'grp')  62.4 us
    dot_general x1, matrix products, per_device(): lax.dot_general(left_rows, right_rows, (((0,), (0,)), ((), ())), preferre...  8.01 us
  transfers between devices with their start and end apart: 3, of which 3 were waited for; matrix products, arithmetic and copies ran while one was open for 0% of the time, Pallas kernels for 0%

commit v1 on v0

--- a/solution.py
+++ b/solution.py
@@ -1,11 +1,16 @@
+import functools
 import math
 
 import jax
 import jax.numpy as jnp
 from jax import lax
+from jax.experimental import pallas as pl
+from jax.experimental.pallas import tpu as pltpu
 from jax.sharding import PartitionSpec as P
 
 R1_WEIGHT = 40.0
+MESH = pl.DeviceIdType.MESH
+TILE = 512
 
 
 def per_device(fake_tokens, real_tokens, proj_weight, score_vector):
@@ -15,10 +20,8 @@
     hid_width = proj_weight.shape[1]
     loss_scale = math.sqrt(hid_width / (lax.axis_size("grp") * lax.axis_size("seq") * tok_count))
     joined = jnp.concatenate([fake_rows, real_rows], 0)
-    shard_rows = lax.all_gather(proj_weight, "seq", axis=0, tiled=True)
-    partial_pre = jnp.dot(joined, shard_rows, preferred_element_type=jnp.float32)
-    full_weight = shard_rows
-    preact, full_weight = (partial_pre, full_weight)
+    full_weight = lax.all_gather(proj_weight, "seq", axis=0, tiled=True)
+    preact = jnp.dot(joined, full_weight, preferred_element_type=jnp.float32)
     squash = jax.nn.sigmoid(preact)
     slopes = squash * (1.0 + preact * (1.0 - squash))
     curves = squash * (1.0 - squash) * (2.0 + preact * (1.0 - 2.0 * squash))
@@ -46,9 +49,303 @@
     return lax.psum(grad_shard, "grp")
 
 
+def kernel(
+    n_z, loss_scale,
+    fake_ref, real_ref, w_ref, score_ref, out_ref,
+    W, joined, tokT, tokP, r1, r1T, r1P, R, RP, slope_s, curve_s, logit,
+    G, rx1, ry1, rx2, ry2, S, rz,
+    w_s, w_r, wp_s, wp_r, tok_s, tok_r, r1_s, r1_r, R_s, R_r, g_s, g_r, z_s, z_r, a_s, a_r,
+):
+    f32 = jnp.float32
+    bf16 = jnp.bfloat16
+    rows, hid = w_ref.shape
+    toks = fake_ref.shape[0]
+    half = TILE // 2
+    g = lax.axis_index("grp")
+    s = lax.axis_index("seq")
+    y, x = g // 2, g % 2
+    z, c = s // 2, s % 2
+    gx, gy, gd = 2 * y + 1 - x, 2 * (1 - y) + x, 3 - g
+    to_x = {"grp": gx, "seq": s}
+    to_y = {"grp": gy, "seq": s}
+    partner = {"grp": g, "seq": 2 * z + 1 - c}
+
+    def to_z(zt):
+        return {"grp": g, "seq": 2 * zt + c}
+
+    barrier = pltpu.get_barrier_semaphore()
+    greet = [to_x, to_y, partner] + [to_z((z + d) % n_z) for d in range(1, n_z)]
+    for dev in greet:
+        pl.semaphore_signal(barrier, inc=1, device_id=dev, device_id_type=MESH)
+    pl.semaphore_wait(barrier, len(greet))
+
+    pending = []
+
+    def send(src, dst, ssem, rsem, dev):
+        cp = pltpu.make_async_remote_copy(
+            src_ref=src, dst_ref=dst, send_sem=ssem, recv_sem=rsem, device_id=dev, device_id_type=MESH
+        )
+        cp.start()
+        pending.append(cp)
+
+    def arrived(ref, rsem):
+        pltpu.make_async_remote_copy(
+            src_ref=ref, dst_ref=ref, send_sem=rsem, recv_sem=rsem, device_id=partner, device_id_type=MESH
+        ).wait_recv()
+
+    def rblk(seq):
+        return pl.ds(pl.multiple_of(rows * seq, 16), rows)
+
+    def quarter(j):
+        return pl.ds(pl.multiple_of(j * TILE, TILE), TILE)
+
+    def halfq(j, h):
+        return pl.ds(pl.multiple_of(j * TILE + h * half, half), half)
+
+    own = rblk(s)
+    for i, d in enumerate(range(1, n_z)):
+        zt = (z + d) % n_z
+        send(w_ref.at[:, quarter(g)], W.at[own, quarter(g)], w_s.at[i, 0], w_r.at[i, 0], to_z(zt))
+    send(w_ref, W.at[own, :], wp_s.at[n_z - 1, 0], wp_r.at[n_z - 1, 0], partner)
+    W[own, :] = w_ref[...]
+    joined[0:toks, :] = fake_ref[...]
+    joined[toks : 2 * toks, :] = real_ref[...]
+
+    @pl.loop(0, joined.shape[1] // TILE)
+    def _(t):
+        cols = pl.ds(pl.multiple_of(t * TILE, TILE), TILE)
+        tokT[cols, :] = joined[:, cols].T
+
+    for b in range(n_z):
+        send(tokT.at[rblk(2 * b + 1 - c), :], tokP.at[b], tok_s.at[b], tok_r.at[b], partner)
+
+    def zrows(i, parity):
+        return rblk(2 * ((z + n_z - 1 - i) % n_z) + parity)
+
+    def stage_a(i):
+        rb = zrows(i, c)
+        mine = W.at[rb, quarter(g)]
+        arrived(mine, w_r.at[i, 0])
+        send(mine, mine, w_s.at[i, 1], w_r.at[i, 1], to_x)
+        send(mine, mine, w_s.at[i, 2], w_r.at[i, 2], to_y)
+        send(mine, mine, wp_s.at[i, 0], wp_r.at[i, 0], partner)
+
+    def stage_b(i):
+        rb = zrows(i, c)
+        ref = W.at[rb, quarter(gx)]
+        arrived(ref, w_r.at[i, 1])
+        h = W.at[rb, halfq(gx, 0)]
+        send(h, h, w_s.at[i, 3], w_r.at[i, 3], to_y)
+        send(ref, ref, wp_s.at[i, 1], wp_r.at[i, 1], partner)
+        ref = W.at[rb, quarter(gy)]
+        arrived(ref, w_r.at[i, 2])
+        h = W.at[rb, halfq(gy, 1)]
+        send(h, h, w_s.at[i, 4], w_r.at[i, 4], to_x)
+        send(ref, ref, wp_s.at[i, 2], wp_r.at[i, 2], partner)
+
+    def stage_c(i):
+        rb = zrows(i, c)
+        arrived(W.at[rb, halfq(gd, 0)], w_r.at[i, 3])
+        arrived(W.at[rb, halfq(gd, 1)], w_r.at[i, 4])
+        ref = W.at[rb, quarter(gd)]
+        send(ref, ref, wp_s.at[i, 3], wp_r.at[i, 3], partner)
+
+    order = [0, 2, 1] if n_z == 4 else list(range(n_z - 1))
+    for k, i in enumerate(order):
+        stage_a(i)
+        if k >= 1:
+            stage_b(order[k - 1])
+        if k >= 2:
+            stage_c(order[k - 2])
+    stage_b(order[-1])
+    for i in order[-2:]:
+        stage_c(i)
+    arrived(W.at[rblk(2 * z + 1 - c), :], wp_r.at[n_z - 1, 0])
+    for i in order:
+        for k, j in enumerate((g, gx, gy, gd)):
+            arrived(W.at[zrows(i, 1 - c), quarter(j)], wp_r.at[i, k])
+
+    logit[...] = jnp.zeros_like(logit)
+
+    @pl.loop(0, hid // TILE)
+    def _(t):
+        cols = pl.ds(pl.multiple_of(t * TILE, TILE), TILE)
+        pre = jnp.dot(joined[...], W[:, cols], preferred_element_type=f32)
+        sv = score_ref[:, cols]
+        sig = 1.0 / (1.0 + jnp.exp(-pre))
+        logit[...] += jnp.sum(pre * sig * sv, axis=1, keepdims=True)
+        sl = sig * (1.0 + pre * (1.0 - sig)) * sv
+        slope_s[:, cols] = sl
+        R[2, :, cols] = sl[toks:].astype(bf16)
+        pr, sr = pre[toks:], sig[toks:]
+        curve_s[:, cols] = sr * (1.0 - sr) * (2.0 + pr * (1.0 - 2.0 * sr)) * sv
+
+    send(R.at[2], RP.at[2], R_s.at[2], R_r.at[2], partner)
+
+    @pl.loop(0, W.shape[0] // TILE)
+    def _(t):
+        cols = pl.ds(pl.multiple_of(t * TILE, TILE), TILE)
+        ig = lax.dot_general(R[2], W[cols, :], (((1,), (1,)), ((), ())), preferred_element_type=f32)
+        r = (loss_scale * R1_WEIGHT * ig).astype(bf16)
+        r1[:, cols] = r
+        r1T[cols, :] = r.T
+
+    for b in range(n_z):
+        send(r1T.at[rblk(2 * b + 1 - c), :], r1P.at[b], r1_s.at[b], r1_r.at[b], partner)
+
+    gate = logit[...]
+    fgate = loss_scale / (1.0 + jnp.exp(-gate[:toks]))
+    rgate = -loss_scale / (1.0 + jnp.exp(gate[toks:]))
+
+    @pl.loop(0, hid // TILE)
+    def _(t):
+        cols = pl.ds(pl.multiple_of(t * TILE, TILE), TILE)
+        R[0, :, cols] = (fgate * slope_s[0:toks, cols]).astype(bf16)
+
+    send(R.at[0], RP.at[0], R_s.at[0], R_r.at[0], partner)
+
+    @pl.loop(0, hid // TILE)
+    def _(t):
+        cols = pl.ds(pl.multiple_of(t * TILE, TILE), TILE)
+        bg = jnp.dot(r1[...], W[:, cols], preferred_element_type=f32)
+        R[1, :, cols] = (rgate * slope_s[toks : 2 * toks, cols] + bg * curve_s[:, cols]).astype(bf16)
+
+    send(R.at[1], RP.at[1], R_s.at[1], R_r.at[1], partner)
+    for b in range(n_z):
+        arrived(tokP.at[b], tok_r.at[b])
+        arrived(r1P.at[b], r1_r.at[b])
+    for b in range(3):
+        arrived(RP.at[b], R_r.at[b])
+
+    def block(k):
+        zb = (z + 1 + k) % n_z
+        mine = rblk(2 * zb + c)
+
+        @pl.loop(0, hid // TILE)
+        def _(t):
+            cols = pl.ds(pl.multiple_of(t * TILE, TILE), TILE)
+            tt = tokT[mine, :]
+            tp = tokP[zb]
+            acc = jnp.dot(tt[:, :toks], R[0, :, cols], preferred_element_type=f32)
+            acc += jnp.dot(tt[:, toks:], R[1, :, cols], preferred_element_type=f32)
+            acc += jnp.dot(r1T[mine, :], R[2, :, cols], preferred_element_type=f32)
+            acc += jnp.dot(tp[:, :toks], RP[0, :, cols], preferred_element_type=f32)
+            acc += jnp.dot(tp[:, toks:], RP[1, :, cols], preferred_element_type=f32)
+            acc += jnp.dot(r1P[zb], RP[2, :, cols], preferred_element_type=f32)
+            G[k, :, cols] = acc
+
+    def step1(k):
+        for m in range(2):
+            send(G.at[k, :, halfq(2 * m + 1 - x, 0)], rx1.at[k, m], g_s.at[k, m], g_r.at[k, m], to_x)
+            send(G.at[k, :, halfq(2 * (1 - y) + m, 1)], ry1.at[k, m], g_s.at[k, 2 + m], g_r.at[k, 2 + m], to_y)
+
+    def step2(k):
+        for m in range(2):
+            arrived(rx1.at[k, m], g_r.at[k, m])
+            arrived(ry1.at[k, m], g_r.at[k, 2 + m])
+        G[k, :, halfq(gy, 0)] += rx1[k, 1 - y]
+        send(G.at[k, :, halfq(gy, 0)], rx2.at[k], g_s.at[k, 4], g_r.at[k, 4], to_y)
+        G[k, :, halfq(gx, 1)] += ry1[k, 1 - x]
+        send(G.at[k, :, halfq(gx, 1)], ry2.at[k], g_s.at[k, 5], g_r.at[k, 5], to_x)
+
+    def step3(k):
+        arrived(rx2.at[k], g_r.at[k, 4])
+        arrived(ry2.at[k], g_r.at[k, 5])
+        S[k, :, 0:half] = G[k, :, halfq(g, 0)] + rx1[k, y] + rx2[k]
+        S[k, :, half:TILE] = G[k, :, halfq(g, 1)] + ry1[k, x] + ry2[k]
+        if k < n_z - 1:
+            send(S.at[k], rz.at[k], z_s.at[k], z_r.at[k], to_z((z + 1 + k) % n_z))
+
+    for k in range(n_z):
+        block(k)
+        step1(k)
+        if k >= 1:
+            step2(k - 1)
+        if k >= 2:
+            step3(k - 2)
+    step2(n_z - 1)
+    for k in range(max(n_z - 2, 0), n_z):
+        step3(k)
+
+    total = S[n_z - 1]
+    for k in range(n_z - 1):
+        arrived(rz.at[k], z_r.at[k])
+        total = total + rz[k]
+    out_ref[:, quarter(g)] = total
+    mine = out_ref.at[:, quarter(g)]
+    send(mine, mine, a_s.at[0], a_r.at[0], to_x)
+    send(mine, mine, a_s.at[1], a_r.at[1], to_y)
+    arrived(out_ref.at[:, quarter(gx)], a_r.at[0])
+    h = out_ref.at[:, halfq(gx, 0)]
+    send(h, h, a_s.at[2], a_r.at[2], to_y)
+    arrived(out_ref.at[:, quarter(gy)], a_r.at[1])
+    h = out_ref.at[:, halfq(gy, 1)]
+    send(h, h, a_s.at[3], a_r.at[3], to_x)
+    arrived(out_ref.at[:, halfq(gd, 0)], a_r.at[2])
+    arrived(out_ref.at[:, halfq(gd, 1)], a_r.at[3])
+    for cp in pending:
+        cp.wait_send()
+
+
+def fused(n_z, loss_scale, fake_tokens, real_tokens, proj_weight, score_vector):
+    toks, d_in = fake_tokens.shape[1:]
+    rows, hid = proj_weight.shape
+    half = TILE // 2
+    f32, bf16 = jnp.float32, jnp.bfloat16
+    vm, dma = pltpu.VMEM, pltpu.SemaphoreType.DMA
+    scratch = [
+        vm((d_in, hid), bf16),
+        vm((2 * toks, d_in), bf16),
+        vm((d_in, 2 * toks), bf16),
+        vm((n_z, rows, 2 * toks), bf16),
+        vm((toks, d_in), bf16),
+        vm((d_in, toks), bf16),
+        vm((n_z, rows, toks), bf16),
+        vm((3, toks, hid), bf16),
+        vm((3, toks, hid), bf16),
+        vm((2 * toks, hid), f32),
+        vm((toks, hid), f32),
+        vm((2 * toks, 1), f32),
+        vm((n_z, rows, hid), f32),
+        vm((n_z, 2, rows, half), f32),
+        vm((n_z, 2, rows, half), f32),
+        vm((n_z, rows, half), f32),
+        vm((n_z, rows, half), f32),
+        vm((n_z, rows, TILE), f32),
+        vm((n_z - 1, rows, TILE), f32),
+        dma((n_z - 1, 5)), dma((n_z - 1, 5)),
+        dma((n_z, 4)), dma((n_z, 4)),
+        dma((n_z,)), dma((n_z,)),
+        dma((n_z,)), dma((n_z,)),
+        dma((3,)), dma((3,)),
+        dma((n_z, 6)), dma((n_z, 6)),
+        dma((n_z - 1,)), dma((n_z - 1,)),
+        dma((4,)), dma((4,)),
+    ]
+    return pl.pallas_call(
+        functools.partial(kernel, n_z, loss_scale),
+        out_shape=jax.ShapeDtypeStruct((rows, hid), f32),
+        in_specs=[pl.BlockSpec(memory_space=pltpu.VMEM)] * 4,
+        out_specs=pl.BlockSpec(memory_space=pltpu.VMEM),
+        scratch_shapes=scratch,
+        compiler_params=pltpu.CompilerParams(
+            collective_id=0, has_side_effects=True, vmem_limit_bytes=58 * 1024 * 1024
+        ),
+    )(fake_tokens[0], real_tokens[0], proj_weight, score_vector[None, :])
+
+
 def solution(mesh):
     in_specs = (P("grp", "seq", None), P("grp", "seq", None), P("seq", None), P())
     out_specs = P("seq", None)
-    return jax.shard_map(
-        per_device, mesh=mesh, in_specs=in_specs, out_specs=out_specs, check_vma=False
-    )
+    n_grp, n_seq = mesh.shape["grp"], mesh.shape["seq"]
+
+    def body(fake_tokens, real_tokens, proj_weight, score_vector):
+        toks = fake_tokens.shape[1]
+        rows, hid = proj_weight.shape
+        fits = n_grp == 4 and n_seq == 8 and hid == 4 * TILE and rows % 16 == 0 and toks % 64 == 0
+        if not fits:
+            return per_device(fake_tokens, real_tokens, proj_weight, score_vector)
+        loss_scale = math.sqrt(hid / (n_grp * n_seq * toks))
+        return fused(n_seq // 2, loss_scale, fake_tokens, real_tokens, proj_weight, score_vector)
+
+    return jax.shard_map(body, mesh=mesh, in_specs=in_specs, out_specs=out_specs, check_vma=False)

time: 298 us -> 135 us (0.45)
  waiting for transfers between devices: 260 us -> 0 us
  Pallas kernels: 0 us -> 132 us
  matrix products: 20.9 us -> 0 us
  between operations: 13.2 us -> 0.01 us
    pallas_call x0 -> x1, Pallas kernels: none -> 132 us  [fused(): pl.pallas_call(functools.partial(kernel, n_z, loss_scale), out_shape=jax....]
    reduce_scatter x1 -> x0, waiting for transfers between devices: 128 us -> none  [per_device(): lax.psum_scatter(grad_term, 'seq', scatter_dimension=0, tiled=True)]
    all_gather x1 -> x0, waiting for transfers between devices: 69.2 us -> none  [per_device(): shard_rows = lax.all_gather(proj_weight, 'seq', axis=0, tiled=True)]
    psum x1 -> x0, waiting for transfers between devices: 62.4 us -> none  [per_device(): return lax.psum(grad_shard, 'grp')]
    dot_general x5 -> x0, matrix products: 20.9 us -> none  [the longest x1 8.01 us: per_device(): lax.dot_general(left_rows, right_rows, (((0,), (0,)), ((), ())), preferre...]
  transfers between devices with their start and end apart: 3 -> 0, of which waited for: 3 -> 0; matrix products, arithmetic and copies ran while one was open for 0% -> 0% of each run, Pallas kernels for 0% -> 0%
where the time goes in v1:
time: 135 us
  Pallas kernels  132 us (98%)
  local copies, waits for them, and re-layouts  2.7 us (2%)
    pallas_call x1, Pallas kernels, fused(): pl.pallas_call(functools.partial(kernel, n_z, loss_scale), out_shape=jax....  132 us
    unnamed x1, local copies, waits for them, and re-layouts  2.7 us

profile of v1, /device:TPU:0, one launch (start us, length us, event | category | flops | bytes accessed | tf_op | source)
XLA Modules:
  0.0 134.5 jit_solution(16359790189148455795)
XLA Ops:
  0.0 131.8 %shard_map.46 = f32[192,2048]{1,0:T(8,128)} custom-call(bf16[192,1536]{1,0:T(8,128)(2,1)} %bitcast.3, bf16[192,1536]{1,0:T(8,128)(2,1)} %bitcast.4, bf16[192,2048]{1,0:T(8,128)(2,1)} %w_ref.1, f32[1,2048]{1,0:T(1,128)} %bitcast.5), custom_call_target="tpu_custom_call" | custom-call | tf_op jit(solution)/shard_map/pallas_call | solution.py:325
  131.8 2.7 %copy.6 = f32[192,2048]{1,0:T(8,128)} copy(f32[192,2048]{1,0:T(8,128)} %shard_map.46) | data formatting | bytes 3145728

commit v2 on v1

v2 whole, which is shorter than its diff:
```python
import functools
import math

import jax
import jax.numpy as jnp
from jax import lax
from jax.experimental import pallas as pl
from jax.experimental.pallas import tpu as pltpu
from jax.sharding import PartitionSpec as P

R1_WEIGHT = 40.0
MESH = pl.DeviceIdType.MESH
TILE = 512


def per_device(fake_tokens, real_tokens, proj_weight, score_vector):
    fake_rows = fake_tokens[0]
    real_rows = real_tokens[0]
    tok_count = fake_rows.shape[0]
    hid_width = proj_weight.shape[1]
    loss_scale = math.sqrt(hid_width / (lax.axis_size("grp") * lax.axis_size("seq") * tok_count))
    joined = jnp.concatenate([fake_rows, real_rows], 0)
    full_weight = lax.all_gather(proj_weight, "seq", axis=0, tiled=True)
    preact = jnp.dot(joined, full_weight, preferred_element_type=jnp.float32)
    squash = jax.nn.sigmoid(preact)
    slopes = squash * (1.0 + preact * (1.0 - squash))
    curves = squash * (1.0 - squash) * (2.0 + preact * (1.0 - 2.0 * squash))
    logits = jnp.dot(preact * squash, score_vector, precision=lax.Precision.HIGHEST)
    slopes_real = slopes[tok_count:]
    lifted = (slopes_real * score_vector).astype(jnp.bfloat16)
    input_grad = lax.dot_general(
        lifted, full_weight, (((1,), (1,)), ((), ())), preferred_element_type=jnp.float32
    )
    r1_cot = (loss_scale * R1_WEIGHT * input_grad).astype(jnp.bfloat16)
    back_grad = jnp.dot(r1_cot, full_weight, preferred_element_type=jnp.float32)
    fake_cot = (
        loss_scale * jax.nn.sigmoid(logits[:tok_count])[:, None] * slopes[:tok_count] * score_vector
    ).astype(jnp.bfloat16)
    real_cot = (
        -loss_scale * jax.nn.sigmoid(-logits[tok_count:])[:, None] * slopes_real * score_vector
        + back_grad * score_vector * curves[tok_count:]
    ).astype(jnp.bfloat16)
    left_rows = jnp.concatenate([fake_rows, real_rows, r1_cot], 0)
    right_rows = jnp.concatenate([fake_cot, real_cot, lifted], 0)
    grad_term = lax.dot_general(
        left_rows, right_rows, (((0,), (0,)), ((), ())), preferred_element_type=jnp.float32
    )
    grad_shard = lax.psum_scatter(grad_term, "seq", scatter_dimension=0, tiled=True)
    return lax.psum(grad_shard, "grp")


def kernel(
    n_z, loss_scale,
    fake_ref, real_ref, w_ref, score_ref, out_ref,
    W, joined, tokT, tokP, ig, r1, r1T, r1P, R, RP, slope_s, curve_s, logit,
    G, rx1, ry1, rx2, ry2, S, rz, zf,
    w_s, w_r, wp_s, wp_r, tok_s, tok_r, r1_s, r1_r, R_s, R_r, g_s, g_r, z_s, z_r, zf_s, zf_r, a_s, a_r,
):
    f32 = jnp.float32
    bf16 = jnp.bfloat16
    rows, hid = w_ref.shape
    toks = fake_ref.shape[0]
    n_tiles = hid // TILE
    sub = TILE // 4
    hr = rows // 2
    zrow = zf.shape[1]
    xr = hr - zrow // 2
    g = lax.axis_index("grp")
    s = lax.axis_index("seq")
    y, x = g // 2, g % 2
    z, c = s // 2, s % 2
    gx, gy, gd = 2 * y + 1 - x, 2 * (1 - y) + x, 3 - g
    to_x = {"grp": gx, "seq": s}
    to_y = {"grp": gy, "seq": s}
    partner = {"grp": g, "seq": 2 * z + 1 - c}

    def to_z(zt):
        return {"grp": g, "seq": 2 * zt + c}

    barrier = pltpu.get_barrier_semaphore()
    greet = [to_x, to_y, partner] + [to_z((z + d) % n_z) for d in range(1, n_z)]
    for dev in greet:
        pl.semaphore_signal(barrier, inc=1, device_id=dev, device_id_type=MESH)
    pl.semaphore_wait(barrier, len(greet))

    pending = []

    def send(src, dst, ssem, rsem, dev):
        cp = pltpu.make_async_remote_copy(
            src_ref=src, dst_ref=dst, send_sem=ssem, recv_sem=rsem, device_id=dev, device_id_type=MESH
        )
        cp.start()
        pending.append(cp)

    def arrived(ref, rsem):
        pltpu.make_async_remote_copy(
            src_ref=ref, dst_ref=ref, send_sem=rsem, recv_sem=rsem, device_id=partner, device_id_type=MESH
        ).wait_recv()

    def rblk(seq):
        return pl.ds(pl.multiple_of(rows * seq, 16), rows)

    def rhalf(seq, h):
        return pl.ds(pl.multiple_of(rows * seq + hr * h, 16), hr)

    def quarter(j):
        return pl.ds(pl.multiple_of(j * TILE, TILE), TILE)

    def subq(t, j):
        return pl.ds(pl.multiple_of(t * TILE + j * sub, sub), sub)

    def tile(t):
        return pl.ds(t * TILE, TILE)

    order = [0, 2, 1] if n_z == 4 else list(range(n_z - 1))
    for t in range(n_tiles):
        for i in order:
            cols = subq(t, g)
            send(
                w_ref.at[:, cols], W.at[rblk(s), cols], w_s.at[t, i, 0], w_r.at[t, i, 0],
                to_z((z + 1 + i) % n_z),
            )
        send(w_ref.at[:, tile(t)], W.at[rblk(s), tile(t)], wp_s.at[t, n_z - 1, 0], wp_r.at[t, n_z - 1, 0], partner)
    W[rblk(s), :] = w_ref[...]
    joined[0:toks, :] = fake_ref[...]
    joined[toks : 2 * toks, :] = real_ref[...]
    ig[...] = jnp.zeros_like(ig)
    logit[...] = jnp.zeros_like(logit)

    @pl.loop(0, joined.shape[1] // TILE)
    def _(t):
        cols = pl.ds(pl.multiple_of(t * TILE, TILE), TILE)
        tokT[cols, :] = joined[:, cols].T

    def zseq(i, parity):
        return 2 * ((z + n_z - 1 - i) % n_z) + parity

    def stage_a(t):
        for i in order:
            mine = W.at[rblk(zseq(i, c)), subq(t, g)]
            arrived(mine, w_r.at[t, i, 0])
            send(mine, mine, w_s.at[t, i, 1], w_r.at[t, i, 1], to_x)
            send(mine, mine, w_s.at[t, i, 2], w_r.at[t, i, 2], to_y)
            send(mine, mine, wp_s.at[t, i, 0], wp_r.at[t, i, 0], partner)

    def stage_b(t):
        for i in order:
            sq = zseq(i, c)
            ref = W.at[rblk(sq), subq(t, gx)]
            arrived(ref, w_r.at[t, i, 1])
            h = W.at[rhalf(sq, 0), subq(t, gx)]
            send(h, h, w_s.at[t, i, 3], w_r.at[t, i, 3], to_y)
            send(ref, ref, wp_s.at[t, i, 1], wp_r.at[t, i, 1], partner)
            ref = W.at[rblk(sq), subq(t, gy)]
            arrived(ref, w_r.at[t, i, 2])
            h = W.at[rhalf(sq, 1), subq(t, gy)]
            send(h, h, w_s.at[t, i, 4], w_r.at[t, i, 4], to_x)
            send(ref, ref, wp_s.at[t, i, 2], wp_r.at[t, i, 2], partner)

    def stage_c(t):
        for i in order:
            sq = zseq(i, c)
            arrived(W.at[rhalf(sq, 0), subq(t, gd)], w_r.at[t, i, 3])
            arrived(W.at[rhalf(sq, 1), subq(t, gd)], w_r.at[t, i, 4])
            ref = W.at[rblk(sq), subq(t, gd)]
            send(ref, ref, wp_s.at[t, i, 3], wp_r.at[t, i, 3], partner)

    def stage_d(t):
        arrived(W.at[rblk(2 * z + 1 - c), tile(t)], wp_r.at[t, n_z - 1, 0])
        for i in order:
            for k, j in enumerate((g, gx, gy, gd)):
                arrived(W.at[rblk(zseq(i, 1 - c)), subq(t, j)], wp_r.at[t, i, k])

    def forward(t):
        cols = tile(t)
        sv = score_ref[:, cols]
        pre = jnp.dot(joined[...], W[:, cols], preferred_element_type=f32)
        sig = 1.0 / (1.0 + jnp.exp(-pre))
        logit[...] += jnp.sum(pre * sig * sv, axis=1, keepdims=True)
        sl = sig * (1.0 + pre * (1.0 - sig)) * sv
        slope_s[:, cols] = sl
        R[2, :, cols] = sl[toks:].astype(bf16)
        pr, sr = pre[toks:], sig[toks:]
        curve_s[:, cols] = sr * (1.0 - sr) * (2.0 + pr * (1.0 - 2.0 * sr)) * sv
        send(R.at[2, :, cols], RP.at[2, :, cols], R_s.at[2, t], R_r.at[2, t], partner)

        @pl.loop(0, W.shape[0] // TILE)
        def _(u):
            ch = pl.ds(pl.multiple_of(u * TILE, TILE), TILE)
            ig[:, ch] += lax.dot_general(
                R[2, :, cols], W[ch, cols], (((1,), (1,)), ((), ())), preferred_element_type=f32
            )

    stage_a(0)
    for b in range(n_z):
        send(tokT.at[rblk(2 * b + 1 - c), :], tokP.at[b], tok_s.at[b], tok_r.at[b], partner)
    stage_b(0)
    for t in range(n_tiles):
        if t + 1 < n_tiles:
            stage_a(t + 1)
        stage_c(t)
        stage_d(t)
        forward(t)
        if t + 1 < n_tiles:
            stage_b(t + 1)

    @pl.loop(0, W.shape[0] // TILE)
    def _(t):
        cols = pl.ds(pl.multiple_of(t * TILE, TILE), TILE)
        r = (loss_scale * R1_WEIGHT * ig[:, cols]).astype(bf16)
        r1[:, cols] = r
        r1T[cols, :] = r.T

    for b in range(n_z):
        send(r1T.at[rblk(2 * b + 1 - c), :], r1P.at[b], r1_s.at[b], r1_r.at[b], partner)

    gate = logit[...]
    fgate = loss_scale / (1.0 + jnp.exp(-gate[:toks]))
    rgate = -loss_scale / (1.0 + jnp.exp(gate[toks:]))
    for t in range(n_tiles):
        cols = tile(t)
        R[0, :, cols] = (fgate * slope_s[0:toks, cols]).astype(bf16)
        send(R.at[0, :, cols], RP.at[0, :, cols], R_s.at[0, t], R_r.at[0, t], partner)
        bg = jnp.dot(r1[...], W[:, cols], preferred_element_type=f32)
        R[1, :, cols] = (rgate * slope_s[toks : 2 * toks, cols] + bg * curve_s[:, cols]).astype(bf16)
        send(R.at[1, :, cols], RP.at[1, :, cols], R_s.at[1, t], R_r.at[1, t], partner)

    for b in range(n_z):
        arrived(tokP.at[b], tok_r.at[b])
        arrived(r1P.at[b], r1_r.at[b])
    for b in range(3):
        for t in range(n_tiles):
            arrived(RP.at[b, :, tile(t)], R_r.at[b, t])

    last = n_z - 1

    def block(k):
        zb = (z + 1 + k) % n_z
        mine = rblk(2 * zb + c)

        @pl.loop(0, n_tiles)
        def _(t):
            cols = pl.ds(pl.multiple_of(t * TILE, TILE), TILE)
            acc = jnp.dot(tokT[mine, :], R[0:2, :, cols].reshape(2 * toks, TILE), preferred_element_type=f32)
            acc += jnp.dot(r1T[mine, :], R[2, :, cols], preferred_element_type=f32)
            acc += jnp.dot(tokP[zb], RP[0:2, :, cols].reshape(2 * toks, TILE), preferred_element_type=f32)
            acc += jnp.dot(r1P[zb], RP[2, :, cols], preferred_element_type=f32)
            G[k, :, cols] = acc

        if k < last:
            send(G.at[k, pl.ds(xr, zrow), :], zf.at[k], zf_s.at[k], zf_r.at[k], to_z(zb))

    def spans(k):
        if k < last:
            return pl.ds(0, xr), pl.ds(xr + zrow, xr), xr
        return pl.ds(0, hr), pl.ds(hr, hr), hr

    def step1(k):
        sx, sy, m = spans(k)
        if k == last:
            for i in range(last):
                arrived(zf.at[i], zf_r.at[i])
            mid = G[k, xr : xr + zrow, :]
            for i in range(last):
                mid = mid + zf[i]
            G[k, xr : xr + zrow, :] = mid
        for j in range(2):
            send(
                G.at[k, sx, quarter(2 * j + 1 - x)], rx1.at[k, j, pl.ds(0, m)],
                g_s.at[k, j], g_r.at[k, j], to_x,
            )
            send(
                G.at[k, sy, quarter(2 * (1 - y) + j)], ry1.at[k, j, pl.ds(0, m)],
                g_s.at[k, 2 + j], g_r.at[k, 2 + j], to_y,
            )

    def step2(k):
        sx, sy, m = spans(k)
        for j in range(2):
            arrived(rx1.at[k, j, pl.ds(0, m)], g_r.at[k, j])
            arrived(ry1.at[k, j, pl.ds(0, m)], g_r.at[k, 2 + j])
        G[k, sx, quarter(gy)] += rx1[k, 1 - y, 0:m]
        send(G.at[k, sx, quarter(gy)], rx2.at[k, pl.ds(0, m)], g_s.at[k, 4], g_r.at[k, 4], to_y)
        G[k, sy, quarter(gx)] += ry1[k, 1 - x, 0:m]
        send(G.at[k, sy, quarter(gx)], ry2.at[k, pl.ds(0, m)], g_s.at[k, 5], g_r.at[k, 5], to_x)

    def step3(k):
        sx, sy, m = spans(k)
        arrived(rx2.at[k, pl.ds(0, m)], g_r.at[k, 4])
        arrived(ry2.at[k, pl.ds(0, m)], g_r.at[k, 5])
        if k < last:
            S[k, 0:m, :] = G[k, sx, quarter(g)] + rx1[k, y, 0:m] + rx2[k, 0:m]
            S[k, m : 2 * m, :] = G[k, sy, quarter(g)] + ry1[k, x, 0:m] + ry2[k, 0:m]
            send(S.at[k], rz.at[k], z_s.at[k], z_r.at[k], to_z((z + 1 + k) % n_z))
        else:
            out_ref[0:m, quarter(g)] = G[k, sx, quarter(g)] + rx1[k, y, 0:m] + rx2[k, 0:m]
            out_ref[m : 2 * m, quarter(g)] = G[k, sy, quarter(g)] + ry1[k, x, 0:m] + ry2[k, 0:m]

    for k in range(n_z):
        block(k)
        if k < last:
            step1(k)
        if k >= 2:
            step2(k - 2)
    step1(last)
    step3(0)
    step2(last - 1)
    for k in range(1, last):
        step3(k)
    step2(last)
    for k in range(last):
        arrived(rz.at[k], z_r.at[k])
    step3(last)
    add = rz[0]
    for k in range(1, last):
        add = add + rz[k]
    out_ref[0:xr, quarter(g)] += add[0:xr]
    out_ref[xr + zrow : rows, quarter(g)] += add[xr : 2 * xr]
    mine = out_ref.at[:, quarter(g)]
    send(mine, mine, a_s.at[0], a_r.at[0], to_x)
    send(mine, mine, a_s.at[1], a_r.at[1], to_y)
    arrived(out_ref.at[:, quarter(gx)], a_r.at[0])
    h = out_ref.at[pl.ds(0, hr), quarter(gx)]
    send(h, h, a_s.at[2], a_r.at[2], to_y)
    arrived(out_ref.at[:, quarter(gy)], a_r.at[1])
    h = out_ref.at[pl.ds(hr, hr), quarter(gy)]
    send(h, h, a_s.at[3], a_r.at[3], to_x)
    arrived(out_ref.at[pl.ds(0, hr), quarter(gd)], a_r.at[2])
    arrived(out_ref.at[pl.ds(hr, hr), quarter(gd)], a_r.at[3])
    for cp in pending:
        cp.wait_send()


def fused(n_z, loss_scale, fake_tokens, real_tokens, proj_weight, score_vector):
    toks, d_in = fake_tokens.shape[1:]
    rows, hid = proj_weight.shape
    f32, bf16 = jnp.float32, jnp.bfloat16
    vm, dma = pltpu.VMEM, pltpu.SemaphoreType.DMA
    tiles = hid // TILE
    hr = rows // 2
    zrow = rows // 6
    xr = hr - zrow // 2
    scratch = [
        vm((d_in, hid), bf16),
        vm((2 * toks, d_in), bf16),
        vm((d_in, 2 * toks), bf16),
        vm((n_z, rows, 2 * toks), bf16),
        vm((toks, d_in), f32),
        vm((toks, d_in), bf16),
        vm((d_in, toks), bf16),
        vm((n_z, rows, toks), bf16),
        vm((3, toks, hid), bf16),
        vm((3, toks, hid), bf16),
        vm((2 * toks, hid), f32),
        vm((toks, hid), f32),
        vm((2 * toks, 1), f32),
        vm((n_z, rows, hid), f32),
        vm((n_z, 2, hr, TILE), f32),
        vm((n_z, 2, hr, TILE), f32),
        vm((n_z, hr, TILE), f32),
        vm((n_z, hr, TILE), f32),
        vm((n_z - 1, 2 * xr, TILE), f32),
        vm((n_z - 1, 2 * xr, TILE), f32),
        vm((n_z - 1, zrow, hid), f32),
        dma((tiles, n_z - 1, 5)), dma((tiles, n_z - 1, 5)),
        dma((tiles, n_z, 4)), dma((tiles, n_z, 4)),
        dma((n_z,)), dma((n_z,)),
        dma((n_z,)), dma((n_z,)),
        dma((3, tiles)), dma((3, tiles)),
        dma((n_z, 6)), dma((n_z, 6)),
        dma((n_z - 1,)), dma((n_z - 1,)),
        dma((n_z - 1,)), dma((n_z - 1,)),
        dma((4,)), dma((4,)),
    ]
    return pl.pallas_call(
        functools.partial(kernel, n_z, loss_scale),
        out_shape=jax.ShapeDtypeStruct((rows, hid), f32),
        in_specs=[pl.BlockSpec(memory_space=pltpu.VMEM)] * 4,
        out_specs=pl.BlockSpec(memory_space=pltpu.VMEM),
        scratch_shapes=scratch,
        compiler_params=pltpu.CompilerParams(
            collective_id=0, has_side_effects=True, vmem_limit_bytes=58 * 1024 * 1024
        ),
    )(fake_tokens[0], real_tokens[0], proj_weight, score_vector[None, :])


def solution(mesh):
    in_specs = (P("grp", "seq", None), P("grp", "seq", None), P("seq", None), P())
    out_specs = P("seq", None)
    n_grp, n_seq = mesh.shape["grp"], mesh.shape["seq"]

    def body(fake_tokens, real_tokens, proj_weight, score_vector):
        toks = fake_tokens.shape[1]
        rows, hid = proj_weight.shape
        fits = n_grp == 4 and n_seq == 8 and hid == 4 * TILE and rows % 96 == 0 and toks % 64 == 0
        if not fits:
            return per_device(fake_tokens, real_tokens, proj_weight, score_vector)
        loss_scale = math.sqrt(hid / (n_grp * n_seq * toks))
        return fused(n_seq // 2, loss_scale, fake_tokens, real_tokens, proj_weight, score_vector)

    return jax.shard_map(body, mesh=mesh, in_specs=in_specs, out_specs=out_specs, check_vma=False)
```

time: 135 us -> 131 us (0.970)
  the two profiles are of different devices: /device:TPU:0 before, /device:TPU:8 now
where the time goes in v2:
time: 131 us; the launch traced here: 130 us
  Pallas kernels  128 us (98%)
  local copies, waits for them, and re-layouts  2.7 us (2%)
    pallas_call x1, Pallas kernels, fused(): pl.pallas_call(functools.partial(kernel, n_z, loss_scale), out_shape=jax....  128 us
    unnamed x1, local copies, waits for them, and re-layouts  2.7 us

profile of v2, /device:TPU:8, one launch (start us, length us, event | category | flops | bytes accessed | tf_op | source)
XLA Modules:
  0.0 130.4 jit_solution(2515053517616103992)
XLA Ops:
  0.0 127.7 %shard_map.46 = f32[192,2048]{1,0:T(8,128)} custom-call(bf16[192,1536]{1,0:T(8,128)(2,1)} %bitcast.3, bf16[192,1536]{1,0:T(8,128)(2,1)} %bitcast.4, bf16[192,2048]{1,0:T(8,128)(2,1)} %w_ref.1, f32[1,2048]{1,0:T(1,128)} %bitcast.5), custom_call_target="tpu_custom_call" | custom-call | tf_op jit(solution)/shard_map/pallas_call | solution.py:375
  127.7 2.7 %copy.6 = f32[192,2048]{1,0:T(8,128)} copy(f32[192,2048]{1,0:T(8,128)} %shard_map.46) | data formatting | bytes 3145728

commit v3 on v2

--- a/solution.py
+++ b/solution.py
@@ -11,6 +11,7 @@
 R1_WEIGHT = 40.0
 MESH = pl.DeviceIdType.MESH
 TILE = 512
+CHUNK = 16
 
 
 def per_device(fake_tokens, real_tokens, proj_weight, score_vector):
@@ -52,7 +53,7 @@
 def kernel(
     n_z, loss_scale,
     fake_ref, real_ref, w_ref, score_ref, out_ref,
-    W, joined, tokT, tokP, ig, r1, r1T, r1P, R, RP, slope_s, curve_s, logit,
+    W, joined, tokT, tokP, igT, liftT, r1, r1T, r1P, R, RP, pre_s, slope_s, curve_s, gate_s,
     G, rx1, ry1, rx2, ry2, S, rz, zf,
     w_s, w_r, wp_s, wp_r, tok_s, tok_r, r1_s, r1_r, R_s, R_r, g_s, g_r, z_s, z_r, zf_s, zf_r, a_s, a_r,
 ):
@@ -120,12 +121,12 @@
                 w_ref.at[:, cols], W.at[rblk(s), cols], w_s.at[t, i, 0], w_r.at[t, i, 0],
                 to_z((z + 1 + i) % n_z),
             )
-        send(w_ref.at[:, tile(t)], W.at[rblk(s), tile(t)], wp_s.at[t, n_z - 1, 0], wp_r.at[t, n_z - 1, 0], partner)
+        send(w_ref.at[:, tile(t)], W.at[rblk(s), tile(t)], wp_s.at[t, n_z - 1], wp_r.at[t, n_z - 1], partner)
     W[rblk(s), :] = w_ref[...]
     joined[0:toks, :] = fake_ref[...]
     joined[toks : 2 * toks, :] = real_ref[...]
-    ig[...] = jnp.zeros_like(ig)
-    logit[...] = jnp.zeros_like(logit)
+    igT[...] = jnp.zeros_like(igT)
+    gate_s[...] = jnp.zeros_like(gate_s)
 
     @pl.loop(0, joined.shape[1] // TILE)
     def _(t):
@@ -141,7 +142,6 @@
             arrived(mine, w_r.at[t, i, 0])
             send(mine, mine, w_s.at[t, i, 1], w_r.at[t, i, 1], to_x)
             send(mine, mine, w_s.at[t, i, 2], w_r.at[t, i, 2], to_y)
-            send(mine, mine, wp_s.at[t, i, 0], wp_r.at[t, i, 0], partner)
 
     def stage_b(t):
         for i in order:
@@ -150,46 +150,61 @@
             arrived(ref, w_r.at[t, i, 1])
             h = W.at[rhalf(sq, 0), subq(t, gx)]
             send(h, h, w_s.at[t, i, 3], w_r.at[t, i, 3], to_y)
-            send(ref, ref, wp_s.at[t, i, 1], wp_r.at[t, i, 1], partner)
             ref = W.at[rblk(sq), subq(t, gy)]
             arrived(ref, w_r.at[t, i, 2])
             h = W.at[rhalf(sq, 1), subq(t, gy)]
             send(h, h, w_s.at[t, i, 4], w_r.at[t, i, 4], to_x)
-            send(ref, ref, wp_s.at[t, i, 2], wp_r.at[t, i, 2], partner)
 
     def stage_c(t):
         for i in order:
             sq = zseq(i, c)
             arrived(W.at[rhalf(sq, 0), subq(t, gd)], w_r.at[t, i, 3])
             arrived(W.at[rhalf(sq, 1), subq(t, gd)], w_r.at[t, i, 4])
-            ref = W.at[rblk(sq), subq(t, gd)]
-            send(ref, ref, wp_s.at[t, i, 3], wp_r.at[t, i, 3], partner)
+            ref = W.at[rblk(sq), tile(t)]
+            send(ref, ref, wp_s.at[t, i], wp_r.at[t, i], partner)
 
     def stage_d(t):
-        arrived(W.at[rblk(2 * z + 1 - c), tile(t)], wp_r.at[t, n_z - 1, 0])
+        arrived(W.at[rblk(2 * z + 1 - c), tile(t)], wp_r.at[t, n_z - 1])
         for i in order:
-            for k, j in enumerate((g, gx, gy, gd)):
-                arrived(W.at[rblk(zseq(i, 1 - c)), subq(t, j)], wp_r.at[t, i, k])
+            arrived(W.at[rblk(zseq(i, 1 - c)), tile(t)], wp_r.at[t, i])
+
+    def lanes(v):
+        out = v[:, 0:128]
+        for q in range(1, TILE // 128):
+            out = out + v[:, 128 * q : 128 * q + 128]
+        return out
 
     def forward(t):
         cols = tile(t)
-        sv = score_ref[:, cols]
-        pre = jnp.dot(joined[...], W[:, cols], preferred_element_type=f32)
-        sig = 1.0 / (1.0 + jnp.exp(-pre))
-        logit[...] += jnp.sum(pre * sig * sv, axis=1, keepdims=True)
-        sl = sig * (1.0 + pre * (1.0 - sig)) * sv
-        slope_s[:, cols] = sl
-        R[2, :, cols] = sl[toks:].astype(bf16)
-        pr, sr = pre[toks:], sig[toks:]
-        curve_s[:, cols] = sr * (1.0 - sr) * (2.0 + pr * (1.0 - 2.0 * sr)) * sv
+        pre_s[...] = jnp.dot(joined[...], W[:, cols], preferred_element_type=f32)
+
+        def common(ch):
+            sv = score_ref[:, cols]
+            pre = pre_s[ch, :]
+            sig = 1.0 / (1.0 + jnp.exp(-pre))
+            gate_s[ch, :] += lanes(pre * sig * sv)
+            sl = sig * (1.0 + pre * (1.0 - sig)) * sv
+            slope_s[ch, cols] = sl
+            return sv, pre, sig, sl
+
+        @pl.loop(0, toks // CHUNK)
+        def _(u):
+            common(pl.ds(pl.multiple_of(u * CHUNK, CHUNK), CHUNK))
+
+        @pl.loop(0, toks // CHUNK)
+        def _(u):
+            ch = pl.ds(pl.multiple_of(u * CHUNK, CHUNK), CHUNK)
+            sv, pre, sig, sl = common(pl.ds(pl.multiple_of(toks + u * CHUNK, CHUNK), CHUNK))
+            R[2, ch, cols] = sl.astype(bf16)
+            curve_s[ch, cols] = sig * (1.0 - sig) * (2.0 + pre * (1.0 - 2.0 * sig)) * sv
+
         send(R.at[2, :, cols], RP.at[2, :, cols], R_s.at[2, t], R_r.at[2, t], partner)
+        liftT[...] = R[2, :, cols].T
 
         @pl.loop(0, W.shape[0] // TILE)
         def _(u):
             ch = pl.ds(pl.multiple_of(u * TILE, TILE), TILE)
-            ig[:, ch] += lax.dot_general(
-                R[2, :, cols], W[ch, cols], (((1,), (1,)), ((), ())), preferred_element_type=f32
-            )
+            igT[ch, :] += jnp.dot(W[ch, cols], liftT[...], preferred_element_type=f32)
 
     stage_a(0)
     for b in range(n_z):
@@ -207,35 +222,45 @@
     @pl.loop(0, W.shape[0] // TILE)
     def _(t):
         cols = pl.ds(pl.multiple_of(t * TILE, TILE), TILE)
-        r = (loss_scale * R1_WEIGHT * ig[:, cols]).astype(bf16)
-        r1[:, cols] = r
-        r1T[cols, :] = r.T
+        r = (loss_scale * R1_WEIGHT * igT[cols, :]).astype(bf16)
+        r1T[cols, :] = r
+        r1[:, cols] = r.T
 
     for b in range(n_z):
         send(r1T.at[rblk(2 * b + 1 - c), :], r1P.at[b], r1_s.at[b], r1_r.at[b], partner)
 
-    gate = logit[...]
-    fgate = loss_scale / (1.0 + jnp.exp(-gate[:toks]))
-    rgate = -loss_scale / (1.0 + jnp.exp(gate[toks:]))
+    gate = jnp.sum(gate_s[...], axis=1, keepdims=True)
+    gate_s[0:toks, :] = jnp.broadcast_to(loss_scale / (1.0 + jnp.exp(-gate[:toks])), (toks, 128))
+    gate_s[toks : 2 * toks, :] = jnp.broadcast_to(-loss_scale / (1.0 + jnp.exp(gate[toks:])), (toks, 128))
+
+    def gated(ch, cols):
+        return jnp.concatenate([gate_s[ch, :]] * (TILE // 128), 1) * slope_s[ch, cols]
+
     for t in range(n_tiles):
         cols = tile(t)
-        R[0, :, cols] = (fgate * slope_s[0:toks, cols]).astype(bf16)
-        send(R.at[0, :, cols], RP.at[0, :, cols], R_s.at[0, t], R_r.at[0, t], partner)
-        bg = jnp.dot(r1[...], W[:, cols], preferred_element_type=f32)
-        R[1, :, cols] = (rgate * slope_s[toks : 2 * toks, cols] + bg * curve_s[:, cols]).astype(bf16)
-        send(R.at[1, :, cols], RP.at[1, :, cols], R_s.at[1, t], R_r.at[1, t], partner)
+        pre_s[0:toks, :] = jnp.dot(r1[...], W[:, cols], preferred_element_type=f32)
+
+        @pl.loop(0, toks // CHUNK)
+        def _(u):
+            ch = pl.ds(pl.multiple_of(u * CHUNK, CHUNK), CHUNK)
+            R[0, ch, cols] = gated(ch, cols).astype(bf16)
+            low = pl.ds(pl.multiple_of(toks + u * CHUNK, CHUNK), CHUNK)
+            R[1, ch, cols] = (gated(low, cols) + pre_s[ch, :] * curve_s[ch, cols]).astype(bf16)
+
+        send(R.at[0:2, :, cols], RP.at[0:2, :, cols], R_s.at[0, t], R_r.at[0, t], partner)
 
     for b in range(n_z):
         arrived(tokP.at[b], tok_r.at[b])
         arrived(r1P.at[b], r1_r.at[b])
-    for b in range(3):
-        for t in range(n_tiles):
-            arrived(RP.at[b, :, tile(t)], R_r.at[b, t])
+    for t in range(n_tiles):
+        arrived(RP.at[2, :, tile(t)], R_r.at[2, t])
+        arrived(RP.at[0:2, :, tile(t)], R_r.at[0, t])
 
     last = n_z - 1
+    hops = [2, 1, 3, 0] if n_z == 4 else [(1 + k) % n_z for k in range(n_z)]
 
     def block(k):
-        zb = (z + 1 + k) % n_z
+        zb = (z + hops[k]) % n_z
         mine = rblk(2 * zb + c)
 
         @pl.loop(0, n_tiles)
@@ -291,7 +316,7 @@
         if k < last:
             S[k, 0:m, :] = G[k, sx, quarter(g)] + rx1[k, y, 0:m] + rx2[k, 0:m]
             S[k, m : 2 * m, :] = G[k, sy, quarter(g)] + ry1[k, x, 0:m] + ry2[k, 0:m]
-            send(S.at[k], rz.at[k], z_s.at[k], z_r.at[k], to_z((z + 1 + k) % n_z))
+            send(S.at[k], rz.at[k], z_s.at[k], z_r.at[k], to_z((z + hops[k]) % n_z))
         else:
             out_ref[0:m, quarter(g)] = G[k, sx, quarter(g)] + rx1[k, y, 0:m] + rx2[k, 0:m]
             out_ref[m : 2 * m, quarter(g)] = G[k, sy, quarter(g)] + ry1[k, x, 0:m] + ry2[k, 0:m]
@@ -331,6 +356,10 @@
         cp.wait_send()
 
 
+def copy_kernel(src_ref, dst_ref):
+    dst_ref[...] = src_ref[...]
+
+
 def fused(n_z, loss_scale, fake_tokens, real_tokens, proj_weight, score_vector):
     toks, d_in = fake_tokens.shape[1:]
     rows, hid = proj_weight.shape
@@ -345,15 +374,17 @@
         vm((2 * toks, d_in), bf16),
         vm((d_in, 2 * toks), bf16),
         vm((n_z, rows, 2 * toks), bf16),
-        vm((toks, d_in), f32),
+        vm((d_in, toks), f32),
+        vm((TILE, toks), bf16),
         vm((toks, d_in), bf16),
         vm((d_in, toks), bf16),
         vm((n_z, rows, toks), bf16),
         vm((3, toks, hid), bf16),
         vm((3, toks, hid), bf16),
+        vm((2 * toks, TILE), f32),
         vm((2 * toks, hid), f32),
         vm((toks, hid), f32),
-        vm((2 * toks, 1), f32),
+        vm((2 * toks, 128), f32),
         vm((n_z, rows, hid), f32),
         vm((n_z, 2, hr, TILE), f32),
         vm((n_z, 2, hr, TILE), f32),
@@ -363,7 +394,7 @@
         vm((n_z - 1, 2 * xr, TILE), f32),
         vm((n_z - 1, zrow, hid), f32),
         dma((tiles, n_z - 1, 5)), dma((tiles, n_z - 1, 5)),
-        dma((tiles, n_z, 4)), dma((tiles, n_z, 4)),
+        dma((tiles, n_z)), dma((tiles, n_z)),
         dma((n_z,)), dma((n_z,)),
         dma((n_z,)), dma((n_z,)),
         dma((3, tiles)), dma((3, tiles)),
@@ -372,7 +403,7 @@
         dma((n_z - 1,)), dma((n_z - 1,)),
         dma((4,)), dma((4,)),
     ]
-    return pl.pallas_call(
+    grad = pl.pallas_call(
         functools.partial(kernel, n_z, loss_scale),
         out_shape=jax.ShapeDtypeStruct((rows, hid), f32),
         in_specs=[pl.BlockSpec(memory_space=pltpu.VMEM)] * 4,
@@ -382,6 +413,10 @@
             collective_id=0, has_side_effects=True, vmem_limit_bytes=58 * 1024 * 1024
         ),
     )(fake_tokens[0], real_tokens[0], proj_weight, score_vector[None, :])
+    spec = pl.BlockSpec((rows // 4, hid), lambda i: (i, 0))
+    return pl.pallas_call(
+        copy_kernel, out_shape=jax.ShapeDtypeStruct((rows, hid), f32), grid=(4,), in_specs=[spec], out_specs=spec
+    )(grad)
 
 
 def solution(mesh):

time: 131 us -> 133 us (1.015)
  the two profiles are of different devices: /device:TPU:8 before, /device:TPU:0 now
where the time goes in v3:
time: 133 us; the launch traced here: 132 us
  Pallas kernels  132 us (99%)
    pallas_call x1, Pallas kernels, fused(): pl.pallas_call(functools.partial(kernel, n_z, loss_scale), out_shape=jax....  129 us
    pallas_call x1, Pallas kernels, fused(): pl.pallas_call(copy_kernel, out_shape=jax.ShapeDtypeStruct((rows, hid), f...  3.57 us

profile of v3, /device:TPU:0, one launch (start us, length us, event | category | flops | bytes accessed | tf_op | source)
XLA Modules:
  0.0 132.4 jit_solution(9960528240487792387)
XLA Ops:
  0.0 128.8 %shard_map.46.src_ref = f32[192,2048]{1,0:T(8,128)} custom-call(bf16[192,1536]{1,0:T(8,128)(2,1)} %bitcast.3, bf16[192,1536]{1,0:T(8,128)(2,1)} %bitcast.4, bf16[192,2048]{1,0:T(8,128)(2,1)} %w_ref.1, f32[1,2048]{1,0:T(1,128)} %bitcast.5), custom_call_target="tpu_custom_call" | custom-call | tf_op jit(solution)/shard_map/pallas_call | solution.py:406
  128.8 3.6 %shard_map.47 = f32[192,2048]{1,0:T(8,128)} custom-call(f32[192,2048]{1,0:T(8,128)} %shard_map.46.src_ref), custom_call_target="tpu_custom_call" | custom-call | tf_op jit(solution)/shard_map/pallas_call | solution.py:417

commit v4 on v3

--- a/solution.py
+++ b/solution.py
@@ -12,6 +12,9 @@
 MESH = pl.DeviceIdType.MESH
 TILE = 512
 CHUNK = 16
+CODED = TILE + TILE // 2
+LEVELS = 21
+STEPS = 2560.0
 
 
 def per_device(fake_tokens, real_tokens, proj_weight, score_vector):
@@ -50,11 +53,29 @@
     return lax.psum(grad_shard, "grp")
 
 
+def encode(v):
+    head = v.astype(jnp.bfloat16)
+    wide = head.astype(jnp.float32)
+    scale = pl.reciprocal(jnp.maximum(jnp.abs(wide), 1e-30), approx=True) * STEPS
+    q = jnp.clip(jnp.round((v - wide) * scale), -(LEVELS // 2), LEVELS // 2)
+    n = v.shape[1] // 2
+    return jnp.concatenate([head, (q[:, :n] * LEVELS + q[:, n:]).astype(jnp.bfloat16)], 1)
+
+
+def decode(e):
+    n = e.shape[1] // 3
+    wide = e[:, : 2 * n].astype(jnp.float32)
+    word = e[:, 2 * n :].astype(jnp.float32)
+    first = jnp.round(word * (1.0 / LEVELS))
+    q = jnp.concatenate([first, word - LEVELS * first], 1)
+    return wide + jnp.abs(wide) * (q * (1.0 / STEPS))
+
+
 def kernel(
     n_z, loss_scale,
     fake_ref, real_ref, w_ref, score_ref, out_ref,
     W, joined, tokT, tokP, igT, liftT, r1, r1T, r1P, R, RP, pre_s, slope_s, curve_s, gate_s,
-    G, rx1, ry1, rx2, ry2, S, rz, zf,
+    G, ex1, ey1, ex2, ey2, rx1, ry1, rx2, ry2, S, rz, ez, zf, A,
     w_s, w_r, wp_s, wp_r, tok_s, tok_r, r1_s, r1_r, R_s, R_r, g_s, g_r, z_s, z_r, zf_s, zf_r, a_s, a_r,
 ):
     f32 = jnp.float32
@@ -64,7 +85,7 @@
     n_tiles = hid // TILE
     sub = TILE // 4
     hr = rows // 2
-    zrow = zf.shape[1]
+    zrow = zf.shape[2]
     xr = hr - zrow // 2
     g = lax.axis_index("grp")
     s = lax.axis_index("seq")
@@ -273,53 +294,109 @@
             G[k, :, cols] = acc
 
         if k < last:
-            send(G.at[k, pl.ds(xr, zrow), :], zf.at[k], zf_s.at[k], zf_r.at[k], to_z(zb))
+            for t in range(n_tiles):
+                for u in range(0, zrow, CHUNK):
+                    ez[k, t, u : u + CHUNK, :] = encode(G[k, xr + u : xr + u + CHUNK, tile(t)])
+            send(ez.at[k], zf.at[k], zf_s.at[k], zf_r.at[k], to_z(zb))
+
+    def over(m, body):
+        @pl.loop(0, m // CHUNK)
+        def _(u):
+            body(pl.multiple_of(u * CHUNK, CHUNK))
+
+    def at(start):
+        return pl.ds(pl.multiple_of(start, CHUNK), CHUNK)
 
     def spans(k):
         if k < last:
-            return pl.ds(0, xr), pl.ds(xr + zrow, xr), xr
-        return pl.ds(0, hr), pl.ds(hr, hr), hr
+            return 0, xr + zrow, xr
+        return 0, hr, hr
 
     def step1(k):
-        sx, sy, m = spans(k)
+        bx, by, m = spans(k)
         if k == last:
             for i in range(last):
                 arrived(zf.at[i], zf_r.at[i])
-            mid = G[k, xr : xr + zrow, :]
-            for i in range(last):
-                mid = mid + zf[i]
-            G[k, xr : xr + zrow, :] = mid
+            for t in range(n_tiles):
+                for u in range(0, zrow, CHUNK):
+                    mid = G[k, xr + u : xr + u + CHUNK, tile(t)]
+                    for i in range(last):
+                        mid = mid + decode(zf[i, t, u : u + CHUNK, :])
+                    G[k, xr + u : xr + u + CHUNK, tile(t)] = mid
         for j in range(2):
-            send(
-                G.at[k, sx, quarter(2 * j + 1 - x)], rx1.at[k, j, pl.ds(0, m)],
-                g_s.at[k, j], g_r.at[k, j], to_x,
-            )
-            send(
-                G.at[k, sy, quarter(2 * (1 - y) + j)], ry1.at[k, j, pl.ds(0, m)],
-                g_s.at[k, 2 + j], g_r.at[k, 2 + j], to_y,
-            )
+            def put_x(r):
+                ex1[k, j, at(r), :] = encode(G[k, at(bx + r), quarter(2 * j + 1 - x)])
+
+            over(m, put_x)
+            part = pl.ds(0, m)
+            send(ex1.at[k, j, part], rx1.at[k, j, part], g_s.at[k, j], g_r.at[k, j], to_x)
+
+            def put_y(r):
+                ey1[k, j, at(r), :] = encode(G[k, at(by + r), quarter(2 * (1 - y) + j)])
+
+            over(m, put_y)
+            send(ey1.at[k, j, part], ry1.at[k, j, part], g_s.at[k, 2 + j], g_r.at[k, 2 + j], to_y)
 
     def step2(k):
-        sx, sy, m = spans(k)
+        bx, by, m = spans(k)
+        part = pl.ds(0, m)
         for j in range(2):
-            arrived(rx1.at[k, j, pl.ds(0, m)], g_r.at[k, j])
-            arrived(ry1.at[k, j, pl.ds(0, m)], g_r.at[k, 2 + j])
-        G[k, sx, quarter(gy)] += rx1[k, 1 - y, 0:m]
-        send(G.at[k, sx, quarter(gy)], rx2.at[k, pl.ds(0, m)], g_s.at[k, 4], g_r.at[k, 4], to_y)
-        G[k, sy, quarter(gx)] += ry1[k, 1 - x, 0:m]
-        send(G.at[k, sy, quarter(gx)], ry2.at[k, pl.ds(0, m)], g_s.at[k, 5], g_r.at[k, 5], to_x)
+            arrived(rx1.at[k, j, part], g_r.at[k, j])
+            arrived(ry1.at[k, j, part], g_r.at[k, 2 + j])
+
+        def put_x(r):
+            ex2[k, at(r), :] = encode(G[k, at(bx + r), quarter(gy)] + decode(rx1[k, 1 - y, at(r), :]))
+
+        over(m, put_x)
+        send(ex2.at[k, part], rx2.at[k, part], g_s.at[k, 4], g_r.at[k, 4], to_y)
+
+        def put_y(r):
+            ey2[k, at(r), :] = encode(G[k, at(by + r), quarter(gx)] + decode(ry1[k, 1 - x, at(r), :]))
+
+        over(m, put_y)
+        send(ey2.at[k, part], ry2.at[k, part], g_s.at[k, 5], g_r.at[k, 5], to_x)
 
     def step3(k):
-        sx, sy, m = spans(k)
+        bx, by, m = spans(k)
         arrived(rx2.at[k, pl.ds(0, m)], g_r.at[k, 4])
         arrived(ry2.at[k, pl.ds(0, m)], g_r.at[k, 5])
+
+        def sum_x(r):
+            return G[k, at(bx + r), quarter(g)] + decode(rx1[k, y, at(r), :]) + decode(rx2[k, at(r), :])
+
+        def sum_y(r):
+            return G[k, at(by + r), quarter(g)] + decode(ry1[k, x, at(r), :]) + decode(ry2[k, at(r), :])
+
         if k < last:
-            S[k, 0:m, :] = G[k, sx, quarter(g)] + rx1[k, y, 0:m] + rx2[k, 0:m]
-            S[k, m : 2 * m, :] = G[k, sy, quarter(g)] + ry1[k, x, 0:m] + ry2[k, 0:m]
+            def put(r):
+                S[k, at(r), :] = encode(sum_x(r))
+                S[k, at(xr + r), :] = encode(sum_y(r))
+
+            over(m, put)
             send(S.at[k], rz.at[k], z_s.at[k], z_r.at[k], to_z((z + hops[k]) % n_z))
         else:
-            out_ref[0:m, quarter(g)] = G[k, sx, quarter(g)] + rx1[k, y, 0:m] + rx2[k, 0:m]
-            out_ref[m : 2 * m, quarter(g)] = G[k, sy, quarter(g)] + ry1[k, x, 0:m] + ry2[k, 0:m]
+            def far(r):
+                out = decode(rz[0, at(r), :])
+                for i in range(1, last):
+                    out = out + decode(rz[i, at(r), :])
+                return out
+
+            def both(r):
+                A[g, at(r), :] = encode(sum_x(r) + far(r))
+                A[g, at(xr + zrow + r), :] = encode(sum_y(xr + zrow - hr + r) + far(xr + r))
+
+            def only(r):
+                A[g, at(xr + r), :] = encode(sum_x(xr + r))
+                A[g, at(hr + r), :] = encode(sum_y(r))
+
+            over(xr, both)
+            over(zrow // 2, only)
+
+    def unpack(j):
+        def put(r):
+            out_ref[at(r), quarter(j)] = decode(A[j, at(r), :])
+
+        over(rows, put)
 
     for k in range(n_z):
         block(k)
@@ -336,28 +413,21 @@
     for k in range(last):
         arrived(rz.at[k], z_r.at[k])
     step3(last)
-    add = rz[0]
-    for k in range(1, last):
-        add = add + rz[k]
-    out_ref[0:xr, quarter(g)] += add[0:xr]
-    out_ref[xr + zrow : rows, quarter(g)] += add[xr : 2 * xr]
-    mine = out_ref.at[:, quarter(g)]
-    send(mine, mine, a_s.at[0], a_r.at[0], to_x)
-    send(mine, mine, a_s.at[1], a_r.at[1], to_y)
-    arrived(out_ref.at[:, quarter(gx)], a_r.at[0])
-    h = out_ref.at[pl.ds(0, hr), quarter(gx)]
-    send(h, h, a_s.at[2], a_r.at[2], to_y)
-    arrived(out_ref.at[:, quarter(gy)], a_r.at[1])
-    h = out_ref.at[pl.ds(hr, hr), quarter(gy)]
-    send(h, h, a_s.at[3], a_r.at[3], to_x)
-    arrived(out_ref.at[pl.ds(0, hr), quarter(gd)], a_r.at[2])
-    arrived(out_ref.at[pl.ds(hr, hr), quarter(gd)], a_r.at[3])
+    send(A.at[g], A.at[g], a_s.at[0], a_r.at[0], to_x)
+    send(A.at[g], A.at[g], a_s.at[1], a_r.at[1], to_y)
+    unpack(g)
+    lo, hi = pl.ds(0, hr), pl.ds(hr, hr)
+    arrived(A.at[gx], a_r.at[0])
+    send(A.at[gx, lo], A.at[gx, lo], a_s.at[2], a_r.at[2], to_y)
+    arrived(A.at[gy], a_r.at[1])
+    send(A.at[gy, hi], A.at[gy, hi], a_s.at[3], a_r.at[3], to_x)
+    unpack(gx)
+    unpack(gy)
+    arrived(A.at[gd, lo], a_r.at[2])
+    arrived(A.at[gd, hi], a_r.at[3])
+    unpack(gd)
     for cp in pending:
         cp.wait_send()
-
-
-def copy_kernel(src_ref, dst_ref):
-    dst_ref[...] = src_ref[...]
 
 
 def fused(n_z, loss_scale, fake_tokens, real_tokens, proj_weight, score_vector):
@@ -386,13 +456,19 @@
         vm((toks, hid), f32),
         vm((2 * toks, 128), f32),
         vm((n_z, rows, hid), f32),
-        vm((n_z, 2, hr, TILE), f32),
-        vm((n_z, 2, hr, TILE), f32),
-        vm((n_z, hr, TILE), f32),
-        vm((n_z, hr, TILE), f32),
-        vm((n_z - 1, 2 * xr, TILE), f32),
-        vm((n_z - 1, 2 * xr, TILE), f32),
-        vm((n_z - 1, zrow, hid), f32),
+        vm((n_z, 2, hr, CODED), bf16),
+        vm((n_z, 2, hr, CODED), bf16),
+        vm((n_z, hr, CODED), bf16),
+        vm((n_z, hr, CODED), bf16),
+        vm((n_z, 2, hr, CODED), bf16),
+        vm((n_z, 2, hr, CODED), bf16),
+        vm((n_z, hr, CODED), bf16),
+        vm((n_z, hr, CODED), bf16),
+        vm((n_z - 1, 2 * xr, CODED), bf16),
+        vm((n_z - 1, 2 * xr, CODED), bf16),
+        vm((n_z - 1, tiles, zrow, CODED), bf16),
+        vm((n_z - 1, tiles, zrow, CODED), bf16),
+        vm((4, rows, CODED), bf16),
         dma((tiles, n_z - 1, 5)), dma((tiles, n_z - 1, 5)),
         dma((tiles, n_z)), dma((tiles, n_z)),
         dma((n_z,)), dma((n_z,)),
@@ -403,7 +479,7 @@
         dma((n_z - 1,)), dma((n_z - 1,)),
         dma((4,)), dma((4,)),
     ]
-    grad = pl.pallas_call(
+    return pl.pallas_call(
         functools.partial(kernel, n_z, loss_scale),
         out_shape=jax.ShapeDtypeStruct((rows, hid), f32),
         in_specs=[pl.BlockSpec(memory_space=pltpu.VMEM)] * 4,
@@ -413,10 +489,6 @@
             collective_id=0, has_side_effects=True, vmem_limit_bytes=58 * 1024 * 1024
         ),
     )(fake_tokens[0], real_tokens[0], proj_weight, score_vector[None, :])
-    spec = pl.BlockSpec((rows // 4, hid), lambda i: (i, 0))
-    return pl.pallas_call(
-        copy_kernel, out_shape=jax.ShapeDtypeStruct((rows, hid), f32), grid=(4,), in_specs=[spec], out_specs=spec
-    )(grad)
 
 
 def solution(mesh):
@@ -427,7 +499,7 @@
     def body(fake_tokens, real_tokens, proj_weight, score_vector):
         toks = fake_tokens.shape[1]
         rows, hid = proj_weight.shape
-        fits = n_grp == 4 and n_seq == 8 and hid == 4 * TILE and rows % 96 == 0 and toks % 64 == 0
+        fits = n_grp == 4 and n_seq == 8 and hid == 4 * TILE and rows % 192 == 0 and toks % 64 == 0
         if not fits:
             return per_device(fake_tokens, real_tokens, proj_weight, score_vector)
         loss_scale = math.sqrt(hid / (n_grp * n_seq * toks))

time: 133 us -> 117 us (0.88)
  Pallas kernels: 132 us -> 114 us
  local copies, waits for them, and re-layouts: 0 us -> 2.7 us
    pallas_call x1, Pallas kernels: 129 us -> 114 us  [fused(): pl.pallas_call(functools.partial(kernel, n_z, loss_scale), out_shape=jax....]
    pallas_call x1 -> x0, Pallas kernels: 3.57 us -> none  [fused(): pl.pallas_call(copy_kernel, out_shape=jax.ShapeDtypeStruct((rows, hid), f...]
    unnamed x0 -> x1, local copies, waits for them, and re-layouts: none -> 2.7 us
where the time goes in v4:
time: 117 us
  Pallas kernels  114 us (97%)
  local copies, waits for them, and re-layouts  2.7 us (2%)
    pallas_call x1, Pallas kernels, fused(): pl.pallas_call(functools.partial(kernel, n_z, loss_scale), out_shape=jax....  114 us
    unnamed x1, local copies, waits for them, and re-layouts  2.7 us

profile of v4, /device:TPU:0, one launch (start us, length us, event | category | flops | bytes accessed | tf_op | source)
XLA Modules:
  0.0 116.6 jit_solution(17867669137343234943)
XLA Ops:
  0.0 113.9 %shard_map.46 = f32[192,2048]{1,0:T(8,128)} custom-call(bf16[192,1536]{1,0:T(8,128)(2,1)} %bitcast.3, bf16[192,1536]{1,0:T(8,128)(2,1)} %bitcast.4, bf16[192,2048]{1,0:T(8,128)(2,1)} %w_ref.1, f32[1,2048]{1,0:T(1,128)} %bitcast.5), custom_call_target="tpu_custom_call" | custom-call | tf_op jit(solution)/shard_map/pallas_call | solution.py:482
  113.9 2.7 %copy.6 = f32[192,2048]{1,0:T(8,128)} copy(f32[192,2048]{1,0:T(8,128)} %shard_map.46) | data formatting | bytes 3145728

commit v5 on v4

--- a/solution.py
+++ b/solution.py
@@ -57,7 +57,7 @@
     head = v.astype(jnp.bfloat16)
     wide = head.astype(jnp.float32)
     scale = pl.reciprocal(jnp.maximum(jnp.abs(wide), 1e-30), approx=True) * STEPS
-    q = jnp.clip(jnp.round((v - wide) * scale), -(LEVELS // 2), LEVELS // 2)
+    q = jnp.round((v - wide) * scale)
     n = v.shape[1] // 2
     return jnp.concatenate([head, (q[:, :n] * LEVELS + q[:, n:]).astype(jnp.bfloat16)], 1)
 
@@ -107,18 +107,24 @@
 
     pending = []
 
-    def send(src, dst, ssem, rsem, dev):
+    def send(src, dst, ssem, rsem, dev, keep=False):
         cp = pltpu.make_async_remote_copy(
             src_ref=src, dst_ref=dst, send_sem=ssem, recv_sem=rsem, device_id=dev, device_id_type=MESH
         )
         cp.start()
-        pending.append(cp)
+        if keep:
+            pending.append(cp)
 
     def arrived(ref, rsem):
         pltpu.make_async_remote_copy(
             src_ref=ref, dst_ref=ref, send_sem=rsem, recv_sem=rsem, device_id=partner, device_id_type=MESH
         ).wait_recv()
 
+    def sent(ref, ssem):
+        pltpu.make_async_remote_copy(
+            src_ref=ref, dst_ref=ref, send_sem=ssem, recv_sem=ssem, device_id=partner, device_id_type=MESH
+        ).wait_send()
+
     def rblk(seq):
         return pl.ds(pl.multiple_of(rows * seq, 16), rows)
 
@@ -132,10 +138,11 @@
         return pl.ds(pl.multiple_of(t * TILE + j * sub, sub), sub)
 
     def tile(t):
-        return pl.ds(t * TILE, TILE)
+        return pl.ds(pl.multiple_of(t * TILE, TILE), TILE)
 
     order = [0, 2, 1] if n_z == 4 else list(range(n_z - 1))
-    for t in range(n_tiles):
+    @pl.loop(0, n_tiles)
+    def _(t):
         for i in order:
             cols = subq(t, g)
             send(
@@ -229,15 +236,21 @@
 
     stage_a(0)
     for b in range(n_z):
-        send(tokT.at[rblk(2 * b + 1 - c), :], tokP.at[b], tok_s.at[b], tok_r.at[b], partner)
+        send(tokT.at[rblk(2 * b + 1 - c), :], tokP.at[b], tok_s.at[b], tok_r.at[b], partner, True)
     stage_b(0)
-    for t in range(n_tiles):
-        if t + 1 < n_tiles:
+
+    @pl.loop(0, n_tiles)
+    def _(t):
+        @pl.when(t + 1 < n_tiles)
+        def _():
             stage_a(t + 1)
+
         stage_c(t)
         stage_d(t)
         forward(t)
-        if t + 1 < n_tiles:
+
+        @pl.when(t + 1 < n_tiles)
+        def _():
             stage_b(t + 1)
 
     @pl.loop(0, W.shape[0] // TILE)
@@ -248,7 +261,7 @@
         r1[:, cols] = r.T
 
     for b in range(n_z):
-        send(r1T.at[rblk(2 * b + 1 - c), :], r1P.at[b], r1_s.at[b], r1_r.at[b], partner)
+        send(r1T.at[rblk(2 * b + 1 - c), :], r1P.at[b], r1_s.at[b], r1_r.at[b], partner, True)
 
     gate = jnp.sum(gate_s[...], axis=1, keepdims=True)
     gate_s[0:toks, :] = jnp.broadcast_to(loss_scale / (1.0 + jnp.exp(-gate[:toks])), (toks, 128))
@@ -257,7 +270,8 @@
     def gated(ch, cols):
         return jnp.concatenate([gate_s[ch, :]] * (TILE // 128), 1) * slope_s[ch, cols]
 
-    for t in range(n_tiles):
+    @pl.loop(0, n_tiles)
+    def _(t):
         cols = tile(t)
         pre_s[0:toks, :] = jnp.dot(r1[...], W[:, cols], preferred_element_type=f32)
 
@@ -273,15 +287,18 @@
     for b in range(n_z):
         arrived(tokP.at[b], tok_r.at[b])
         arrived(r1P.at[b], r1_r.at[b])
-    for t in range(n_tiles):
+    @pl.loop(0, n_tiles)
+    def _(t):
         arrived(RP.at[2, :, tile(t)], R_r.at[2, t])
         arrived(RP.at[0:2, :, tile(t)], R_r.at[0, t])
 
     last = n_z - 1
-    hops = [2, 1, 3, 0] if n_z == 4 else [(1 + k) % n_z for k in range(n_z)]
-
-    def block(k):
-        zb = (z + hops[k]) % n_z
+
+    def hop(k):
+        return (z + 1 + k) % n_z
+
+    def block(k, own=False):
+        zb = hop(k)
         mine = rblk(2 * zb + c)
 
         @pl.loop(0, n_tiles)
@@ -293,10 +310,12 @@
             acc += jnp.dot(r1P[zb], RP[2, :, cols], preferred_element_type=f32)
             G[k, :, cols] = acc
 
-        if k < last:
-            for t in range(n_tiles):
+        if not own:
+            @pl.loop(0, n_tiles)
+            def _(t):
                 for u in range(0, zrow, CHUNK):
                     ez[k, t, u : u + CHUNK, :] = encode(G[k, xr + u : xr + u + CHUNK, tile(t)])
+
             send(ez.at[k], zf.at[k], zf_s.at[k], zf_r.at[k], to_z(zb))
 
     def over(m, body):
@@ -307,17 +326,19 @@
     def at(start):
         return pl.ds(pl.multiple_of(start, CHUNK), CHUNK)
 
-    def spans(k):
-        if k < last:
+    def spans(own):
+        if not own:
             return 0, xr + zrow, xr
         return 0, hr, hr
 
-    def step1(k):
-        bx, by, m = spans(k)
-        if k == last:
+    def step1(k, own=False):
+        bx, by, m = spans(own)
+        if own:
             for i in range(last):
                 arrived(zf.at[i], zf_r.at[i])
-            for t in range(n_tiles):
+
+            @pl.loop(0, n_tiles)
+            def _(t):
                 for u in range(0, zrow, CHUNK):
                     mid = G[k, xr + u : xr + u + CHUNK, tile(t)]
                     for i in range(last):
@@ -337,8 +358,8 @@
             over(m, put_y)
             send(ey1.at[k, j, part], ry1.at[k, j, part], g_s.at[k, 2 + j], g_r.at[k, 2 + j], to_y)
 
-    def step2(k):
-        bx, by, m = spans(k)
+    def step2(k, own=False):
+        bx, by, m = spans(own)
         part = pl.ds(0, m)
         for j in range(2):
             arrived(rx1.at[k, j, part], g_r.at[k, j])
@@ -356,8 +377,8 @@
         over(m, put_y)
         send(ey2.at[k, part], ry2.at[k, part], g_s.at[k, 5], g_r.at[k, 5], to_x)
 
-    def step3(k):
-        bx, by, m = spans(k)
+    def step3(k, own=False):
+        bx, by, m = spans(own)
         arrived(rx2.at[k, pl.ds(0, m)], g_r.at[k, 4])
         arrived(ry2.at[k, pl.ds(0, m)], g_r.at[k, 5])
 
@@ -367,13 +388,13 @@
         def sum_y(r):
             return G[k, at(by + r), quarter(g)] + decode(ry1[k, x, at(r), :]) + decode(ry2[k, at(r), :])
 
-        if k < last:
+        if not own:
             def put(r):
                 S[k, at(r), :] = encode(sum_x(r))
                 S[k, at(xr + r), :] = encode(sum_y(r))
 
             over(m, put)
-            send(S.at[k], rz.at[k], z_s.at[k], z_r.at[k], to_z((z + hops[k]) % n_z))
+            send(S.at[k], rz.at[k], z_s.at[k], z_r.at[k], to_z(hop(k)))
         else:
             def far(r):
                 out = decode(rz[0, at(r), :])
@@ -398,29 +419,38 @@
 
         over(rows, put)
 
-    for k in range(n_z):
+    @pl.loop(0, last)
+    def _(k):
         block(k)
-        if k < last:
-            step1(k)
-        if k >= 2:
-            step2(k - 2)
-    step1(last)
-    step3(0)
-    step2(last - 1)
-    for k in range(1, last):
+        step1(k)
+
+        @pl.when(k >= 1)
+        def _():
+            step2(k - 1)
+
+    block(last, True)
+    step1(last, True)
+
+    @pl.loop(0, last)
+    def _(k):
+        @pl.when(k == 1)
+        def _():
+            step2(last - 1)
+
         step3(k)
-    step2(last)
+
+    step2(last, True)
     for k in range(last):
         arrived(rz.at[k], z_r.at[k])
-    step3(last)
-    send(A.at[g], A.at[g], a_s.at[0], a_r.at[0], to_x)
-    send(A.at[g], A.at[g], a_s.at[1], a_r.at[1], to_y)
+    step3(last, True)
+    send(A.at[g], A.at[g], a_s.at[0], a_r.at[0], to_x, True)
+    send(A.at[g], A.at[g], a_s.at[1], a_r.at[1], to_y, True)
     unpack(g)
     lo, hi = pl.ds(0, hr), pl.ds(hr, hr)
     arrived(A.at[gx], a_r.at[0])
-    send(A.at[gx, lo], A.at[gx, lo], a_s.at[2], a_r.at[2], to_y)
+    send(A.at[gx, lo], A.at[gx, lo], a_s.at[2], a_r.at[2], to_y, True)
     arrived(A.at[gy], a_r.at[1])
-    send(A.at[gy, hi], A.at[gy, hi], a_s.at[3], a_r.at[3], to_x)
+    send(A.at[gy, hi], A.at[gy, hi], a_s.at[3], a_r.at[3], to_x, True)
     unpack(gx)
     unpack(gy)
     arrived(A.at[gd, lo], a_r.at[2])
@@ -428,6 +458,35 @@
     unpack(gd)
     for cp in pending:
         cp.wait_send()
+
+    @pl.loop(0, n_tiles)
+    def _(t):
+        for i in order:
+            for m in range(3):
+                sent(W.at[0:rows, 0:sub], w_s.at[t, i, m])
+            for m in range(3, 5):
+                sent(W.at[0:hr, 0:sub], w_s.at[t, i, m])
+        for i in range(n_z):
+            sent(W.at[0:rows, 0:TILE], wp_s.at[t, i])
+        sent(R.at[2, :, tile(t)], R_s.at[2, t])
+        sent(R.at[0:2, :, tile(t)], R_s.at[0, t])
+
+    def drain(k, own=False):
+        part = pl.ds(0, spans(own)[2])
+        for j in range(2):
+            sent(ex1.at[k, j, part], g_s.at[k, j])
+            sent(ey1.at[k, j, part], g_s.at[k, 2 + j])
+        sent(ex2.at[k, part], g_s.at[k, 4])
+        sent(ey2.at[k, part], g_s.at[k, 5])
+        if not own:
+            sent(ez.at[k], zf_s.at[k])
+            sent(S.at[k], z_s.at[k])
+
+    @pl.loop(0, last)
+    def _(k):
+        drain(k)
+
+    drain(last, True)
 
 
 def fused(n_z, loss_scale, fake_tokens, real_tokens, proj_weight, score_vector):

time: 117 us -> 115 us (0.983)
  Pallas kernels: 114 us -> 112 us
    pallas_call x1, Pallas kernels: 114 us -> 112 us  [fused(): pl.pallas_call(functools.partial(kernel, n_z, loss_scale), out_shape=jax....]
where the time goes in v5:
time: 115 us
  Pallas kernels  112 us (97%)
  local copies, waits for them, and re-layouts  2.7 us (2%)
    pallas_call x1, Pallas kernels, fused(): pl.pallas_call(functools.partial(kernel, n_z, loss_scale), out_shape=jax....  112 us
    unnamed x1, local copies, waits for them, and re-layouts  2.7 us

profile of v5, /device:TPU:0, one launch (start us, length us, event | category | flops | bytes accessed | tf_op | source)
XLA Modules:
  0.0 114.6 jit_solution(1275049997072095148)
XLA Ops:
  0.0 111.9 %shard_map.46 = f32[192,2048]{1,0:T(8,128)} custom-call(bf16[192,1536]{1,0:T(8,128)(2,1)} %bitcast.3, bf16[192,1536]{1,0:T(8,128)(2,1)} %bitcast.4, bf16[192,2048]{1,0:T(8,128)(2,1)} %w_ref.1, f32[1,2048]{1,0:T(1,128)} %bitcast.5), custom_call_target="tpu_custom_call" | custom-call | tf_op jit(solution)/shard_map/pallas_call | solution.py:541
  111.9 2.7 %copy.6 = f32[192,2048]{1,0:T(8,128)} copy(f32[192,2048]{1,0:T(8,128)} %shard_map.46) | data formatting | bytes 3145728

commit v6 on v5

--- a/solution.py
+++ b/solution.py
@@ -74,7 +74,7 @@
 def kernel(
     n_z, loss_scale,
     fake_ref, real_ref, w_ref, score_ref, out_ref,
-    W, joined, tokT, tokP, igT, liftT, r1, r1T, r1P, R, RP, pre_s, slope_s, curve_s, gate_s,
+    W, joined, tokT, L, igT, liftT, r1, r1T, R, pre_s, slope_s, curve_s, gate_s,
     G, ex1, ey1, ex2, ey2, rx1, ry1, rx2, ry2, S, rz, ez, zf, A,
     w_s, w_r, wp_s, wp_r, tok_s, tok_r, r1_s, r1_r, R_s, R_r, g_s, g_r, z_s, z_r, zf_s, zf_r, a_s, a_r,
 ):
@@ -83,6 +83,8 @@
     rows, hid = w_ref.shape
     toks = fake_ref.shape[0]
     n_tiles = hid // TILE
+    pad = r1T.shape[1]
+    lift, lift_p = 4 * toks, 4 * toks + pad
     sub = TILE // 4
     hr = rows // 2
     zrow = zf.shape[2]
@@ -125,6 +127,9 @@
             src_ref=ref, dst_ref=ref, send_sem=ssem, recv_sem=ssem, device_id=partner, device_id_type=MESH
         ).wait_send()
 
+    def hop(k):
+        return (z + 1 + k) % n_z
+
     def rblk(seq):
         return pl.ds(pl.multiple_of(rows * seq, 16), rows)
 
@@ -154,6 +159,9 @@
     joined[0:toks, :] = fake_ref[...]
     joined[toks : 2 * toks, :] = real_ref[...]
     igT[...] = jnp.zeros_like(igT)
+    r1T[:, toks:pad] = jnp.zeros((r1T.shape[0], pad - toks), bf16)
+    R[lift + toks : lift_p, :] = jnp.zeros((pad - toks, hid), bf16)
+    R[lift_p + toks : lift_p + pad, :] = jnp.zeros((pad - toks, hid), bf16)
     gate_s[...] = jnp.zeros_like(gate_s)
 
     @pl.loop(0, joined.shape[1] // TILE)
@@ -223,11 +231,12 @@
         def _(u):
             ch = pl.ds(pl.multiple_of(u * CHUNK, CHUNK), CHUNK)
             sv, pre, sig, sl = common(pl.ds(pl.multiple_of(toks + u * CHUNK, CHUNK), CHUNK))
-            R[2, ch, cols] = sl.astype(bf16)
+            R[pl.ds(pl.multiple_of(lift + u * CHUNK, CHUNK), CHUNK), cols] = sl.astype(bf16)
             curve_s[ch, cols] = sig * (1.0 - sig) * (2.0 + pre * (1.0 - 2.0 * sig)) * sv
 
-        send(R.at[2, :, cols], RP.at[2, :, cols], R_s.at[2, t], R_r.at[2, t], partner)
-        liftT[...] = R[2, :, cols].T
+        made = R.at[lift : lift + toks, cols]
+        send(made, R.at[lift_p : lift_p + toks, cols], R_s.at[1, t], R_r.at[1, t], partner)
+        liftT[...] = made[...].T
 
         @pl.loop(0, W.shape[0] // TILE)
         def _(u):
@@ -236,7 +245,11 @@
 
     stage_a(0)
     for b in range(n_z):
-        send(tokT.at[rblk(2 * b + 1 - c), :], tokP.at[b], tok_s.at[b], tok_r.at[b], partner, True)
+        send(
+            tokT.at[rblk(2 * hop(b) + 1 - c), :], L.at[b, :, 2 * toks : 4 * toks],
+            tok_s.at[b], tok_r.at[b], partner, True,
+        )
+        L[b, :, 0 : 2 * toks] = tokT[rblk(2 * hop(b) + c), :]
     stage_b(0)
 
     @pl.loop(0, n_tiles)
@@ -257,11 +270,15 @@
     def _(t):
         cols = pl.ds(pl.multiple_of(t * TILE, TILE), TILE)
         r = (loss_scale * R1_WEIGHT * igT[cols, :]).astype(bf16)
-        r1T[cols, :] = r
+        r1T[cols, 0:toks] = r
         r1[:, cols] = r.T
 
     for b in range(n_z):
-        send(r1T.at[rblk(2 * b + 1 - c), :], r1P.at[b], r1_s.at[b], r1_r.at[b], partner, True)
+        send(
+            r1T.at[rblk(2 * hop(b) + 1 - c), :], L.at[b, :, lift_p : lift_p + pad],
+            r1_s.at[b], r1_r.at[b], partner, True,
+        )
+        L[b, :, lift:lift_p] = r1T[rblk(2 * hop(b) + c), :]
 
     gate = jnp.sum(gate_s[...], axis=1, keepdims=True)
     gate_s[0:toks, :] = jnp.broadcast_to(loss_scale / (1.0 + jnp.exp(-gate[:toks])), (toks, 128))
@@ -278,48 +295,41 @@
         @pl.loop(0, toks // CHUNK)
         def _(u):
             ch = pl.ds(pl.multiple_of(u * CHUNK, CHUNK), CHUNK)
-            R[0, ch, cols] = gated(ch, cols).astype(bf16)
+            R[ch, cols] = gated(ch, cols).astype(bf16)
             low = pl.ds(pl.multiple_of(toks + u * CHUNK, CHUNK), CHUNK)
-            R[1, ch, cols] = (gated(low, cols) + pre_s[ch, :] * curve_s[ch, cols]).astype(bf16)
-
-        send(R.at[0:2, :, cols], RP.at[0:2, :, cols], R_s.at[0, t], R_r.at[0, t], partner)
+            R[low, cols] = (gated(low, cols) + pre_s[ch, :] * curve_s[ch, cols]).astype(bf16)
+
+        send(R.at[0 : 2 * toks, cols], R.at[2 * toks : 4 * toks, cols], R_s.at[0, t], R_r.at[0, t], partner)
 
     for b in range(n_z):
-        arrived(tokP.at[b], tok_r.at[b])
-        arrived(r1P.at[b], r1_r.at[b])
+        arrived(L.at[b, :, 2 * toks : 4 * toks], tok_r.at[b])
+        arrived(L.at[b, :, lift_p : lift_p + pad], r1_r.at[b])
     @pl.loop(0, n_tiles)
     def _(t):
-        arrived(RP.at[2, :, tile(t)], R_r.at[2, t])
-        arrived(RP.at[0:2, :, tile(t)], R_r.at[0, t])
+        arrived(R.at[lift_p : lift_p + toks, tile(t)], R_r.at[1, t])
+        arrived(R.at[2 * toks : 4 * toks, tile(t)], R_r.at[0, t])
 
     last = n_z - 1
 
-    def hop(k):
-        return (z + 1 + k) % n_z
-
-    def block(k, own=False):
-        zb = hop(k)
-        mine = rblk(2 * zb + c)
+    def products(p):
+        two = pl.ds(2 * p, 2)
 
         @pl.loop(0, n_tiles)
         def _(t):
-            cols = pl.ds(pl.multiple_of(t * TILE, TILE), TILE)
-            acc = jnp.dot(tokT[mine, :], R[0:2, :, cols].reshape(2 * toks, TILE), preferred_element_type=f32)
-            acc += jnp.dot(r1T[mine, :], R[2, :, cols], preferred_element_type=f32)
-            acc += jnp.dot(tokP[zb], RP[0:2, :, cols].reshape(2 * toks, TILE), preferred_element_type=f32)
-            acc += jnp.dot(r1P[zb], RP[2, :, cols], preferred_element_type=f32)
-            G[k, :, cols] = acc
-
-        if not own:
-            @pl.loop(0, n_tiles)
-            def _(t):
-                for u in range(0, zrow, CHUNK):
-                    ez[k, t, u : u + CHUNK, :] = encode(G[k, xr + u : xr + u + CHUNK, tile(t)])
-
-            send(ez.at[k], zf.at[k], zf_s.at[k], zf_r.at[k], to_z(zb))
+            cols = tile(t)
+            left = L[two].reshape(2 * rows, L.shape[2])
+            G[two, :, cols] = jnp.dot(left, R[:, cols], preferred_element_type=f32).reshape(2, rows, TILE)
+
+    def far_rows(k):
+        @pl.loop(0, n_tiles)
+        def _(t):
+            for u in range(0, zrow, CHUNK):
+                ez[k, t, u : u + CHUNK, :] = encode(G[k, xr + u : xr + u + CHUNK, tile(t)])
+
+        send(ez.at[k], zf.at[k], zf_s.at[k], zf_r.at[k], to_z(hop(k)))
 
     def over(m, body):
-        @pl.loop(0, m // CHUNK)
+        @pl.loop(0, m // CHUNK, unroll=True)
         def _(u):
             body(pl.multiple_of(u * CHUNK, CHUNK))
 
@@ -421,14 +431,17 @@
 
     @pl.loop(0, last)
     def _(k):
-        block(k)
+        @pl.when(k % 2 == 0)
+        def _():
+            products(k // 2)
+
+        far_rows(k)
         step1(k)
 
-        @pl.when(k >= 1)
-        def _():
-            step2(k - 1)
-
-    block(last, True)
+    @pl.loop(0, last - 1)
+    def _(k):
+        step2(k)
+
     step1(last, True)
 
     @pl.loop(0, last)
@@ -468,8 +481,8 @@
                 sent(W.at[0:hr, 0:sub], w_s.at[t, i, m])
         for i in range(n_z):
             sent(W.at[0:rows, 0:TILE], wp_s.at[t, i])
-        sent(R.at[2, :, tile(t)], R_s.at[2, t])
-        sent(R.at[0:2, :, tile(t)], R_s.at[0, t])
+        sent(R.at[0:toks, tile(t)], R_s.at[1, t])
+        sent(R.at[0 : 2 * toks, tile(t)], R_s.at[0, t])
 
     def drain(k, own=False):
         part = pl.ds(0, spans(own)[2])
@@ -495,6 +508,7 @@
     f32, bf16 = jnp.float32, jnp.bfloat16
     vm, dma = pltpu.VMEM, pltpu.SemaphoreType.DMA
     tiles = hid // TILE
+    pad = -(-toks // 128) * 128
     hr = rows // 2
     zrow = rows // 6
     xr = hr - zrow // 2
@@ -502,14 +516,12 @@
         vm((d_in, hid), bf16),
         vm((2 * toks, d_in), bf16),
         vm((d_in, 2 * toks), bf16),
-        vm((n_z, rows, 2 * toks), bf16),
+        vm((n_z, rows, 4 * toks + 2 * pad), bf16),
         vm((d_in, toks), f32),
         vm((TILE, toks), bf16),
         vm((toks, d_in), bf16),
-        vm((d_in, toks), bf16),
-        vm((n_z, rows, toks), bf16),
-        vm((3, toks, hid), bf16),
-        vm((3, toks, hid), bf16),
+        vm((d_in, pad), bf16),
+        vm((4 * toks + 2 * pad, hid), bf16),
         vm((2 * toks, TILE), f32),
         vm((2 * toks, hid), f32),
         vm((toks, hid), f32),
@@ -532,7 +544,7 @@
         dma((tiles, n_z)), dma((tiles, n_z)),
         dma((n_z,)), dma((n_z,)),
         dma((n_z,)), dma((n_z,)),
-        dma((3, tiles)), dma((3, tiles)),
+        dma((2, tiles)), dma((2, tiles)),
         dma((n_z, 6)), dma((n_z, 6)),
         dma((n_z - 1,)), dma((n_z - 1,)),
         dma((n_z - 1,)), dma((n_z - 1,)),

time: 115 us -> 117 us (1.017); the launches traced: 115 us -> 115 us
  no operation moved by 1% of the time
where the time goes in v6:
time: 117 us; the launch traced here: 115 us
  Pallas kernels  112 us (96%)
  local copies, waits for them, and re-layouts  2.7 us (2%)
    pallas_call x1, Pallas kernels, fused(): pl.pallas_call(functools.partial(kernel, n_z, loss_scale), out_shape=jax....  112 us
    unnamed x1, local copies, waits for them, and re-layouts  2.7 us

profile of v6, /device:TPU:0, one launch (start us, length us, event | category | flops | bytes accessed | tf_op | source)
XLA Modules:
  0.0 114.9 jit_solution(10861156732460737797)
XLA Ops:
  0.0 112.2 %shard_map.46 = f32[192,2048]{1,0:T(8,128)} custom-call(bf16[192,1536]{1,0:T(8,128)(2,1)} %bitcast.3, bf16[192,1536]{1,0:T(8,128)(2,1)} %bitcast.4, bf16[192,2048]{1,0:T(8,128)(2,1)} %w_ref.1, f32[1,2048]{1,0:T(1,128)} %bitcast.5), custom_call_target="tpu_custom_call" | custom-call | tf_op jit(solution)/shard_map/pallas_call | solution.py:553
  112.2 2.7 %copy.6 = f32[192,2048]{1,0:T(8,128)} copy(f32[192,2048]{1,0:T(8,128)} %shard_map.46) | data formatting | bytes 3145728

commit v7 on v5

--- a/solution.py
+++ b/solution.py
@@ -83,7 +83,8 @@
     rows, hid = w_ref.shape
     toks = fake_ref.shape[0]
     n_tiles = hid // TILE
-    sub = TILE // 4
+    sub = rows // 4
+    cut = sub // 48 * 16 if sub % 48 == 0 else sub // 32 * 16
     hr = rows // 2
     zrow = zf.shape[2]
     xr = hr - zrow // 2
@@ -128,14 +129,16 @@
     def rblk(seq):
         return pl.ds(pl.multiple_of(rows * seq, 16), rows)
 
-    def rhalf(seq, h):
-        return pl.ds(pl.multiple_of(rows * seq + hr * h, 16), hr)
-
     def quarter(j):
         return pl.ds(pl.multiple_of(j * TILE, TILE), TILE)
 
-    def subq(t, j):
-        return pl.ds(pl.multiple_of(t * TILE + j * sub, sub), sub)
+    def part_of(seq, j):
+        return pl.ds(pl.multiple_of(rows * seq + sub * j, 16), sub)
+
+    def cut_of(seq, j, i, h):
+        first = cut if i % 2 == 0 else sub - cut
+        size = first if h == 0 else sub - first
+        return pl.ds(pl.multiple_of(rows * seq + sub * j + h * first, 16), size)
 
     def tile(t):
         return pl.ds(pl.multiple_of(t * TILE, TILE), TILE)
@@ -144,13 +147,14 @@
     @pl.loop(0, n_tiles)
     def _(t):
         for i in order:
-            cols = subq(t, g)
+            mine = pl.ds(pl.multiple_of(sub * g, 16), sub)
             send(
-                w_ref.at[:, cols], W.at[rblk(s), cols], w_s.at[t, i, 0], w_r.at[t, i, 0],
+                w_ref.at[mine, tile(t)], W.at[t, part_of(s, g), :], w_s.at[t, i, 0], w_r.at[t, i, 0],
                 to_z((z + 1 + i) % n_z),
             )
-        send(w_ref.at[:, tile(t)], W.at[rblk(s), tile(t)], wp_s.at[t, n_z - 1], wp_r.at[t, n_z - 1], partner)
-    W[rblk(s), :] = w_ref[...]
+        send(w_ref.at[:, tile(t)], W.at[t, rblk(s), :], wp_s.at[t, n_z - 1], wp_r.at[t, n_z - 1], partner)
+    for t in range(n_tiles):
+        W[t, rblk(s), :] = w_ref[:, t * TILE : (t + 1) * TILE]
     joined[0:toks, :] = fake_ref[...]
     joined[toks : 2 * toks, :] = real_ref[...]
     igT[...] = jnp.zeros_like(igT)
@@ -166,7 +170,7 @@
 
     def stage_a(t):
         for i in order:
-            mine = W.at[rblk(zseq(i, c)), subq(t, g)]
+            mine = W.at[t, part_of(zseq(i, c), g), :]
             arrived(mine, w_r.at[t, i, 0])
             send(mine, mine, w_s.at[t, i, 1], w_r.at[t, i, 1], to_x)
             send(mine, mine, w_s.at[t, i, 2], w_r.at[t, i, 2], to_y)
@@ -174,27 +178,27 @@
     def stage_b(t):
         for i in order:
             sq = zseq(i, c)
-            ref = W.at[rblk(sq), subq(t, gx)]
+            ref = W.at[t, part_of(sq, gx), :]
             arrived(ref, w_r.at[t, i, 1])
-            h = W.at[rhalf(sq, 0), subq(t, gx)]
+            h = W.at[t, cut_of(sq, gx, i, 0), :]
             send(h, h, w_s.at[t, i, 3], w_r.at[t, i, 3], to_y)
-            ref = W.at[rblk(sq), subq(t, gy)]
+            ref = W.at[t, part_of(sq, gy), :]
             arrived(ref, w_r.at[t, i, 2])
-            h = W.at[rhalf(sq, 1), subq(t, gy)]
+            h = W.at[t, cut_of(sq, gy, i, 1), :]
             send(h, h, w_s.at[t, i, 4], w_r.at[t, i, 4], to_x)
 
     def stage_c(t):
         for i in order:
             sq = zseq(i, c)
-            arrived(W.at[rhalf(sq, 0), subq(t, gd)], w_r.at[t, i, 3])
-            arrived(W.at[rhalf(sq, 1), subq(t, gd)], w_r.at[t, i, 4])
-            ref = W.at[rblk(sq), tile(t)]
+            arrived(W.at[t, cut_of(sq, gd, i, 0), :], w_r.at[t, i, 3])
+            arrived(W.at[t, cut_of(sq, gd, i, 1), :], w_r.at[t, i, 4])
+            ref = W.at[t, rblk(sq), :]
             send(ref, ref, wp_s.at[t, i], wp_r.at[t, i], partner)
 
     def stage_d(t):
-        arrived(W.at[rblk(2 * z + 1 - c), tile(t)], wp_r.at[t, n_z - 1])
+        arrived(W.at[t, rblk(2 * z + 1 - c), :], wp_r.at[t, n_z - 1])
         for i in order:
-            arrived(W.at[rblk(zseq(i, 1 - c)), tile(t)], wp_r.at[t, i])
+            arrived(W.at[t, rblk(zseq(i, 1 - c)), :], wp_r.at[t, i])
 
     def lanes(v):
         out = v[:, 0:128]
@@ -204,7 +208,7 @@
 
     def forward(t):
         cols = tile(t)
-        pre_s[...] = jnp.dot(joined[...], W[:, cols], preferred_element_type=f32)
+        pre_s[...] = jnp.dot(joined[...], W[t], preferred_element_type=f32)
 
         def common(ch):
             sv = score_ref[:, cols]
@@ -229,10 +233,10 @@
         send(R.at[2, :, cols], RP.at[2, :, cols], R_s.at[2, t], R_r.at[2, t], partner)
         liftT[...] = R[2, :, cols].T
 
-        @pl.loop(0, W.shape[0] // TILE)
+        @pl.loop(0, W.shape[1] // TILE)
         def _(u):
             ch = pl.ds(pl.multiple_of(u * TILE, TILE), TILE)
-            igT[ch, :] += jnp.dot(W[ch, cols], liftT[...], preferred_element_type=f32)
+            igT[ch, :] += jnp.dot(W[t, ch, :], liftT[...], preferred_element_type=f32)
 
     stage_a(0)
     for b in range(n_z):
@@ -253,7 +257,7 @@
         def _():
             stage_b(t + 1)
 
-    @pl.loop(0, W.shape[0] // TILE)
+    @pl.loop(0, W.shape[1] // TILE)
     def _(t):
         cols = pl.ds(pl.multiple_of(t * TILE, TILE), TILE)
         r = (loss_scale * R1_WEIGHT * igT[cols, :]).astype(bf16)
@@ -273,7 +277,7 @@
     @pl.loop(0, n_tiles)
     def _(t):
         cols = tile(t)
-        pre_s[0:toks, :] = jnp.dot(r1[...], W[:, cols], preferred_element_type=f32)
+        pre_s[0:toks, :] = jnp.dot(r1[...], W[t], preferred_element_type=f32)
 
         @pl.loop(0, toks // CHUNK)
         def _(u):
@@ -463,11 +467,11 @@
     def _(t):
         for i in order:
             for m in range(3):
-                sent(W.at[0:rows, 0:sub], w_s.at[t, i, m])
-            for m in range(3, 5):
-                sent(W.at[0:hr, 0:sub], w_s.at[t, i, m])
+                sent(W.at[t, 0:sub, :], w_s.at[t, i, m])
+            for h in range(2):
+                sent(W.at[t, cut_of(0, 0, i, h), :], w_s.at[t, i, 3 + h])
         for i in range(n_z):
-            sent(W.at[0:rows, 0:TILE], wp_s.at[t, i])
+            sent(W.at[t, 0:rows, :], wp_s.at[t, i])
         sent(R.at[2, :, tile(t)], R_s.at[2, t])
         sent(R.at[0:2, :, tile(t)], R_s.at[0, t])
 
@@ -499,7 +503,7 @@
     zrow = rows // 6
     xr = hr - zrow // 2
     scratch = [
-        vm((d_in, hid), bf16),
+        vm((tiles, d_in, TILE), bf16),
         vm((2 * toks, d_in), bf16),
         vm((d_in, 2 * toks), bf16),
         vm((n_z, rows, 2 * toks), bf16),

time: 115 us -> 116 us (level)
  no operation moved by 1% of the time
where the time goes in v7:
time: 116 us; the launch traced here: 115 us
  Pallas kernels  113 us (97%)
  local copies, waits for them, and re-layouts  2.7 us (2%)
    pallas_call x1, Pallas kernels, fused(): pl.pallas_call(functools.partial(kernel, n_z, loss_scale), out_shape=jax....  113 us
    unnamed x1, local copies, waits for them, and re-layouts  2.7 us

profile of v7, /device:TPU:0, one launch (start us, length us, event | category | flops | bytes accessed | tf_op | source)
XLA Modules:
  0.0 115.3 jit_solution(7740029841966609565)
XLA Ops:
  0.0 112.6 %shard_map.46 = f32[192,2048]{1,0:T(8,128)} custom-call(bf16[192,1536]{1,0:T(8,128)(2,1)} %bitcast.3, bf16[192,1536]{1,0:T(8,128)(2,1)} %bitcast.4, bf16[192,2048]{1,0:T(8,128)(2,1)} %w_ref.1, f32[1,2048]{1,0:T(1,128)} %bitcast.5), custom_call_target="tpu_custom_call" | custom-call | tf_op jit(solution)/shard_map/pallas_call | solution.py:545
  112.6 2.7 %copy.6 = f32[192,2048]{1,0:T(8,128)} copy(f32[192,2048]{1,0:T(8,128)} %shard_map.46) | data formatting | bytes 3145728

commit v8 on v5

--- a/solution.py
+++ b/solution.py
@@ -75,8 +75,8 @@
     n_z, loss_scale,
     fake_ref, real_ref, w_ref, score_ref, out_ref,
     W, joined, tokT, tokP, igT, liftT, r1, r1T, r1P, R, RP, pre_s, slope_s, curve_s, gate_s,
-    G, ex1, ey1, ex2, ey2, rx1, ry1, rx2, ry2, S, rz, ez, zf, A,
-    w_s, w_r, wp_s, wp_r, tok_s, tok_r, r1_s, r1_r, R_s, R_r, g_s, g_r, z_s, z_r, zf_s, zf_r, a_s, a_r,
+    G, ex1, ey1, ex2, ey2, rx1, ry1, rx2, ry2, S, rz, A,
+    w_s, w_r, wp_s, wp_r, tok_s, tok_r, r1_s, r1_r, R_s, R_r, g_s, g_r, z_s, z_r, a_s, a_r,
 ):
     f32 = jnp.float32
     bf16 = jnp.bfloat16
@@ -85,8 +85,7 @@
     n_tiles = hid // TILE
     sub = TILE // 4
     hr = rows // 2
-    zrow = zf.shape[2]
-    xr = hr - zrow // 2
+    zrow, xr = 0, hr
     g = lax.axis_index("grp")
     s = lax.axis_index("seq")
     y, x = g // 2, g % 2
@@ -310,14 +309,6 @@
             acc += jnp.dot(r1P[zb], RP[2, :, cols], preferred_element_type=f32)
             G[k, :, cols] = acc
 
-        if not own:
-            @pl.loop(0, n_tiles)
-            def _(t):
-                for u in range(0, zrow, CHUNK):
-                    ez[k, t, u : u + CHUNK, :] = encode(G[k, xr + u : xr + u + CHUNK, tile(t)])
-
-            send(ez.at[k], zf.at[k], zf_s.at[k], zf_r.at[k], to_z(zb))
-
     def over(m, body):
         @pl.loop(0, m // CHUNK)
         def _(u):
@@ -333,17 +324,6 @@
 
     def step1(k, own=False):
         bx, by, m = spans(own)
-        if own:
-            for i in range(last):
-                arrived(zf.at[i], zf_r.at[i])
-
-            @pl.loop(0, n_tiles)
-            def _(t):
-                for u in range(0, zrow, CHUNK):
-                    mid = G[k, xr + u : xr + u + CHUNK, tile(t)]
-                    for i in range(last):
-                        mid = mid + decode(zf[i, t, u : u + CHUNK, :])
-                    G[k, xr + u : xr + u + CHUNK, tile(t)] = mid
         for j in range(2):
             def put_x(r):
                 ex1[k, j, at(r), :] = encode(G[k, at(bx + r), quarter(2 * j + 1 - x)])
@@ -406,12 +386,7 @@
                 A[g, at(r), :] = encode(sum_x(r) + far(r))
                 A[g, at(xr + zrow + r), :] = encode(sum_y(xr + zrow - hr + r) + far(xr + r))
 
-            def only(r):
-                A[g, at(xr + r), :] = encode(sum_x(xr + r))
-                A[g, at(hr + r), :] = encode(sum_y(r))
-
             over(xr, both)
-            over(zrow // 2, only)
 
     def unpack(j):
         def put(r):
@@ -479,7 +454,6 @@
         sent(ex2.at[k, part], g_s.at[k, 4])
         sent(ey2.at[k, part], g_s.at[k, 5])
         if not own:
-            sent(ez.at[k], zf_s.at[k])
             sent(S.at[k], z_s.at[k])
 
     @pl.loop(0, last)
@@ -496,8 +470,7 @@
     vm, dma = pltpu.VMEM, pltpu.SemaphoreType.DMA
     tiles = hid // TILE
     hr = rows // 2
-    zrow = rows // 6
-    xr = hr - zrow // 2
+    xr = hr
     scratch = [
         vm((d_in, hid), bf16),
         vm((2 * toks, d_in), bf16),
@@ -525,8 +498,6 @@
         vm((n_z, hr, CODED), bf16),
         vm((n_z - 1, 2 * xr, CODED), bf16),
         vm((n_z - 1, 2 * xr, CODED), bf16),
-        vm((n_z - 1, tiles, zrow, CODED), bf16),
-        vm((n_z - 1, tiles, zrow, CODED), bf16),
         vm((4, rows, CODED), bf16),
         dma((tiles, n_z - 1, 5)), dma((tiles, n_z - 1, 5)),
         dma((tiles, n_z)), dma((tiles, n_z)),
@@ -534,7 +505,6 @@
         dma((n_z,)), dma((n_z,)),
         dma((3, tiles)), dma((3, tiles)),
         dma((n_z, 6)), dma((n_z, 6)),
-        dma((n_z - 1,)), dma((n_z - 1,)),
         dma((n_z - 1,)), dma((n_z - 1,)),
         dma((4,)), dma((4,)),
     ]

time: 115 us -> 120 us (1.043)
  Pallas kernels: 112 us -> 117 us
    pallas_call x1, Pallas kernels: 112 us -> 117 us  [fused(): pl.pallas_call(functools.partial(kernel, n_z, loss_scale), out_shape=jax....]
where the time goes in v8:
time: 120 us; the launch traced here: 119 us
  Pallas kernels  117 us (98%)
  local copies, waits for them, and re-layouts  2.7 us (2%)
    pallas_call x1, Pallas kernels, fused(): pl.pallas_call(functools.partial(kernel, n_z, loss_scale), out_shape=jax....  117 us
    unnamed x1, local copies, waits for them, and re-layouts  2.7 us

profile of v8, /device:TPU:0, one launch (start us, length us, event | category | flops | bytes accessed | tf_op | source)
XLA Modules:
  0.0 119.3 jit_solution(4432086764151723825)
XLA Ops:
  0.0 116.5 %shard_map.46 = f32[192,2048]{1,0:T(8,128)} custom-call(bf16[192,1536]{1,0:T(8,128)(2,1)} %bitcast.3, bf16[192,1536]{1,0:T(8,128)(2,1)} %bitcast.4, bf16[192,2048]{1,0:T(8,128)(2,1)} %w_ref.1, f32[1,2048]{1,0:T(1,128)} %bitcast.5), custom_call_target="tpu_custom_call" | custom-call | tf_op jit(solution)/shard_map/pallas_call | solution.py:511
  116.5 2.7 %copy.6 = f32[192,2048]{1,0:T(8,128)} copy(f32[192,2048]{1,0:T(8,128)} %shard_map.46) | data formatting | bytes 3145728
